TPU v7x, 256 devices: a whole 4x4x8 slice. The times are simulated.
256 devices in a mesh: expert: 32 (over z, y), tensor: 8 (over x, core).
Axes of the slice: x: 4, y: 4, z: 8, core: 2. Of those that a mesh axis runs over, the one named last changes fastest.
Arguments:
- frames: bfloat16 [4096, 1536], P('expert'), may hold values from -6 to 6
- cotangent: bfloat16 [4096, 1536], P('expert'), may hold values from -6 to 6
- segment_ids: int32 [4096], P('expert'), may hold values from 0 to 2, as said below
- kernel: float32 [31, 1536], replicated, may hold values from -1 to 1
- expert_ids: int32 [4096, 2], P('expert'), may hold values from 0 to 31, all different within a row; in each aligned block of 128 rows (0 to 127, 128 to 255, ...) at most 16 rows name the same one
- gates: bfloat16 [4096, 2], P('expert'), may hold values from 0.099609375 to 1
- w_in: bfloat16 [32, 1536, 6144], P('expert', None, 'tensor'), may hold values from -0.15625 to 0.15625
- w_out: bfloat16 [32, 6144, 1536], P('expert', 'tensor'), may hold values from -0.078125 to 0.078125
Outputs:
- frames_grad: bfloat16 [4096, 1536], P('expert')
- kernel_grad: float32 [31, 1536], replicated
- w_in_grad: bfloat16 [32, 1536, 6144], P('expert', None, 'tensor')
- w_out_grad: bfloat16 [32, 6144, 1536], P('expert', 'tensor')
- gate_grad: float32 [4096, 2], P('expert')
Inputs may be any that keep to these rules, and one draw needn't show every extreme that they name: `expert_ids`: within the 128 frames of one index of expert, no expert is chosen more than 16 times. `segment_ids`: never falling along the frames; three utterances, the first ending before frame 4096 // 4 and the last starting at frame 3 * 1024 or later.
All inputs are finite; a program needn't handle non-finite values.
Results may differ from a plain program's by a relative error of at most 0.011.
Values may be sent and summed in bfloat16 or wider, within the bound.
A program may use at most 128 MiB of HBM per device.

v0:
```python
import jax
import jax.numpy as jnp
from jax import lax
from jax.sharding import PartitionSpec as P


def extended(value, sides, width):
    for axis, dim in sides:
        devices, length = (lax.axis_size(axis), value.shape[dim])
        up = [(i, (i + 1) % devices) for i in range(devices - 1)]
        down = [(j, i) for i, j in up]
        last = lax.slice_in_dim(value, length - width, length, axis=dim)
        leading = lax.slice_in_dim(value, 0, width, axis=dim)
        before = lax.ppermute(last, axis, up)
        after = lax.ppermute(leading, axis, down)
        value = jnp.concatenate([before, value, after], axis=dim)
    return value


def on_device(frames, cotangent, segment_ids, kernel, expert_ids, gates, w_in, w_out):
    n_expert = lax.axis_size("expert")
    count = frames.shape[0]
    width = frames.shape[1]
    top = expert_ids.shape[1]
    kernel_len = kernel.shape[0]
    pad = kernel_len // 2
    capacity = max(2, 4 * count // n_expert)
    slots = n_expert * capacity
    flat_count = count * top
    frame_edge, seg_edge = (
        extended(frames, (("expert", 0),), pad),
        extended(segment_ids.astype(jnp.bfloat16), (("expert", 0),), pad),
    )
    own_seg = segment_ids.astype(jnp.bfloat16)
    inputs = frames.astype(jnp.float32)
    conv = jnp.zeros_like(inputs)
    masks = []
    for j in range(kernel_len):
        mask = (seg_edge[j : j + count] == own_seg).astype(jnp.float32)
        masks.append(mask)
        conv = (
            conv
            + kernel[j][None, :] * frame_edge[j : j + count].astype(jnp.float32) * mask[:, None]
        )
    mixed = (inputs + conv).astype(jnp.bfloat16)
    chosen = expert_ids.reshape(-1)
    onehot = (chosen[:, None] == jnp.arange(n_expert, dtype=jnp.int32)[None, :]).astype(jnp.int32)
    rank = jnp.sum((jnp.cumsum(onehot, axis=0) - onehot) * onehot, axis=1)
    position = chosen * capacity + rank
    source = (
        jnp.full((slots,), flat_count, jnp.int32)
        .at[position]
        .set(jnp.arange(flat_count, dtype=jnp.int32))
    )
    zero_row = jnp.zeros((1, width), jnp.bfloat16)
    mixed_rows = jnp.concatenate([jnp.repeat(mixed, top, axis=0), zero_row], 0)[source]
    grad_rows = jnp.concatenate([jnp.repeat(cotangent, top, axis=0), zero_row], 0)[source]
    gate_rows = jnp.concatenate([gates.reshape(-1), jnp.zeros((1,), jnp.bfloat16)], 0)[source]
    mixed_blocks = mixed_rows.reshape(n_expert, capacity, width)
    grad_blocks = grad_rows.reshape(n_expert, capacity, width)
    gate_blocks = gate_rows.reshape(n_expert, capacity)
    rows_in, rows_grad, weight = (
        lax.all_to_all(mixed_blocks, "expert", split_axis=0, concat_axis=0, tiled=True),
        lax.all_to_all(grad_blocks, "expert", split_axis=0, concat_axis=0, tiled=True),
        lax.all_to_all(gate_blocks, "expert", split_axis=0, concat_axis=0, tiled=True),
    )
    rows_in = rows_in.reshape(slots, width)
    rows_grad = rows_grad.reshape(slots, width)
    weight = weight.reshape(slots).astype(jnp.float32)[:, None]
    first = w_in[0]
    second = w_out[0]
    pre = jnp.dot(rows_in, first, preferred_element_type=jnp.float32)
    sig = jax.nn.sigmoid(pre)
    hidden = (pre * sig).astype(jnp.bfloat16)
    scaled = (weight * rows_grad.astype(jnp.float32)).astype(jnp.bfloat16)
    back = jnp.dot(rows_grad, second.T, preferred_element_type=jnp.float32)
    pre_grad = (back * weight * (sig * (1.0 + pre * (1.0 - sig)))).astype(jnp.bfloat16)
    gate_part = jnp.sum(hidden.astype(jnp.float32) * back, axis=1)
    first_grad = jnp.dot(rows_in.T, pre_grad, preferred_element_type=jnp.float32).astype(
        jnp.bfloat16
    )
    second_grad = jnp.dot(hidden.T, scaled, preferred_element_type=jnp.float32).astype(jnp.bfloat16)
    input_part = jnp.dot(pre_grad, first.T, preferred_element_type=jnp.float32)
    share = lax.psum_scatter(
        input_part.reshape(n_expert, capacity, width).astype(jnp.bfloat16),
        "tensor",
        scatter_dimension=2,
        tiled=True,
    ).astype(jnp.float32)
    gate_total = lax.psum(gate_part.reshape(n_expert, capacity), "tensor")
    back_share, back_gate = (
        lax.all_to_all(share, "expert", split_axis=0, concat_axis=0, tiled=True),
        lax.all_to_all(gate_total, "expert", split_axis=0, concat_axis=0, tiled=True),
    )
    columns = back_share.shape[2]
    picked = back_share.reshape(slots, columns)[position].reshape(count, top, columns)
    moe_grad = lax.all_gather(jnp.sum(picked, axis=1), "tensor", axis=1, tiled=True)
    gate_grad = back_gate.reshape(slots)[position].reshape(count, top)
    mixed_grad = cotangent.astype(jnp.float32) + moe_grad
    grad_edge = extended(mixed_grad, (("expert", 0),), pad)
    kernel_rows = []
    transposed = jnp.zeros_like(mixed_grad)
    for j in range(kernel_len):
        kernel_rows.append(
            jnp.sum(
                mixed_grad * frame_edge[j : j + count].astype(jnp.float32) * masks[j][:, None],
                axis=0,
            )
        )
        start = 2 * pad - j
        mask = (seg_edge[start : start + count] == own_seg).astype(jnp.float32)
        transposed = (
            transposed + kernel[j][None, :] * grad_edge[start : start + count] * mask[:, None]
        )
    kernel_grad = lax.psum(jnp.stack(kernel_rows, 0), "expert")
    frames_grad = (mixed_grad + transposed).astype(jnp.bfloat16)
    return (frames_grad, kernel_grad, first_grad[None], second_grad[None], gate_grad)


def solution(mesh):
    return jax.shard_map(
        on_device,
        mesh=mesh,
        in_specs=(
            P("expert", None),
            P("expert", None),
            P("expert"),
            P(),
            P("expert", None),
            P("expert", None),
            P("expert", None, "tensor"),
            P("expert", "tensor", None),
        ),
        out_specs=(
            P("expert", None),
            P(),
            P("expert", None, "tensor"),
            P("expert", "tensor", None),
            P("expert", None),
        ),
        check_vma=False,
    )
```

profile of v0, /device:TPU:2, one launch (start us, length us, event | category | flops | bytes accessed | tf_op | source)
XLA Modules:
  0.0 483.0 jit_solution(1383158990264330792)
XLA Ops:
  8.7 4.0 collective-permute-start.1
  19.4 3.5 gather_fusion.1
  23.6 12.9 %all-to-all-start.1 = ((bf16[32,1,16]{2,1,0:T(2,128)(2,1)}), bf16[32,1,16]{2,1,0:T(2,128)(2,1)}, u32[]{:S(2)}, u32[]{:S(2)}) async-start(bf16[32,1,16]{2,1,0:T(2,128)(2,1)} %all_to_all.28), calls=%async_computation.1 | async-start | bytes 32768 | tf_op jit(solution)/shard_map/all_to_all | solution.py:65
  40.5 4.6 collective-permute-start
  52.9 15.9 %fusion.251 = bf16[128,1536]{0,1:T(8,128)(2,1)} fusion(bf16[128,1536]{0,1:T(8,128)(2,1)S(1)} %copy.42, f32[128]{0:T(128)S(1)} %get-tuple-element.105, f32[1536]{0:T(1024)} %get-tuple-element.80, f32[128]{0:T(128)S(1)} %get-tuple-element.106, f32[1536]{0:T(1024)} %get-tuple-element.81, f32[128]{0:T(128)S(1)} %get-tuple-element.107, ...), kind=kLoop, calls=%fused_computation.443 | loop fusion | flops 42270720 | bytes 1084928 | tf_op jit(solution)/shard_map/convert_element_type | solution.py:45
  73.0 3.0 reshape.146
  77.1 2.9 gather_fusion.2
  80.1 13.8 %all-to-all-start.2 = ((bf16[32,16,1536]{2,1,0:T(8,128)(2,1)}), bf16[32,16,1536]{2,1,0:T(8,128)(2,1)}, u32[]{:S(2)}, u32[]{:S(2)}) async-start(bf16[32,16,1536]{2,1,0:T(8,128)(2,1)} %bitcast.54), calls=%async_computation.2 | async-start | bytes 3145728 | tf_op jit(solution)/shard_map/all_to_all | solution.py:63
  96.7 2.9 gather_fusion
  99.6 31.0 %all-to-all-done.2 = bf16[32,16,1536]{2,1,0:T(8,128)(2,1)} async-done(((bf16[32,16,1536]{2,1,0:T(8,128)(2,1)}), bf16[32,16,1536]{2,1,0:T(8,128)(2,1)}, u32[]{:S(2)}, u32[]{:S(2)}) %all-to-all-start.2) | async-done | bytes 1572896 | tf_op jit(solution)/shard_map/all_to_all | solution.py:63
  130.6 5.9 %all-to-all-start = ((bf16[32,16,1536]{2,1,0:T(8,128)(2,1)}), bf16[32,16,1536]{2,1,0:T(8,128)(2,1)}, u32[]{:S(2)}, u32[]{:S(2)}) async-start(bf16[32,16,1536]{2,1,0:T(8,128)(2,1)} %bitcast.55), calls=%async_computation | async-start | bytes 3145728 | tf_op jit(solution)/shard_map/all_to_all | solution.py:64
  137.4 3.9 fusion.3
  141.3 31.6 %all-to-all-done = bf16[32,16,1536]{2,1,0:T(8,128)(2,1)} async-done(((bf16[32,16,1536]{2,1,0:T(8,128)(2,1)}), bf16[32,16,1536]{2,1,0:T(8,128)(2,1)}, u32[]{:S(2)}, u32[]{:S(2)}) %all-to-all-start) | async-done | bytes 1572896 | tf_op jit(solution)/shard_map/all_to_all | solution.py:64
  172.9 4.4 multiply_reduce_fusion
  180.9 18.0 %copy.56 = bf16[32,16,1536]{1,0,2:T(8,128)(2,1)} copy(bf16[32,16,1536]{2,1,0:T(8,128)(2,1)} %convolution_convert_fusion.2) | data formatting | bytes 3145728
  198.8 21.9 %reshape.208 = bf16[1536,512]{1,0:T(8,128)(2,1)} reshape(bf16[1536,32,16]{2,1,0:T(8,128)(2,1)} %bitcast.51) | data formatting | bytes 3145728
  220.8 20.8 %psum.15 = f32[32,1,16]{2,0,1:T(8,128)} all-reduce(f32[32,1,16]{2,0,1:T(8,128)S(1)} %all_to_all.26), channel_id=1, replica_groups=mesh['expert'=32,'tensor'=8] {'tensor'}, use_global_device_ids=true, to_apply=%region_39.40 | all-reduce | flops 512 | bytes 4096 | tf_op jit(solution)/shard_map/psum | solution.py:90
  241.7 5.9 %all-to-all-start.4 = ((f32[32,1,16]{2,1,0:T(1,128)}), f32[32,1,16]{2,1,0:T(1,128)S(1)}, u32[]{:S(2)}, u32[]{:S(2)}) async-start(f32[32,1,16]{2,1,0:T(1,128)} %bitcast.14), calls=%async_computation.4 | async-start | bytes 32768 | tf_op jit(solution)/shard_map/all_to_all | solution.py:93
  250.2 3.0 reshape.209
  257.3 9.0 %all-to-all-start.3 = ((f32[32,16,192]{2,1,0:T(8,128)}), f32[32,16,192]{2,1,0:T(8,128)S(1)}, u32[]{:S(2)}, u32[]{:S(2)}) async-start(f32[32,16,192]{2,1,0:T(8,128)} %convert_element_type.377), calls=%async_computation.3 | async-start | bytes 1048576 | tf_op jit(solution)/shard_map/all_to_all | solution.py:92
  266.3 4.6 fusion
  270.8 4.4 fusion.1
  279.3 4.3 all-to-all-done.3
  285.1 14.6 %all_gather.3 = f32[128,1536]{0,1:T(8,128)S(1)} all-gather(f32[128,192]{0,1:T(8,128)S(1)} %copy.48), channel_id=1, replica_groups=mesh['expert'=32,'tensor'=8] {'tensor'}, dimensions={1}, use_global_device_ids=true | all-gather | bytes 884736 | tf_op jit(solution)/shard_map/all_gather | solution.py:97
  299.8 5.3 %fusion.127 = (f32[1536]{0:T(1024)}, f32[1536]{0:T(1024)}, f32[1536]{0:T(1024)}, f32[1536]{0:T(1024)}, f32[1536]{0:T(1024)}, /*index=5*/f32[1536]{0:T(1024)}, f32[128,1536]{0,1:T(8,128)S(1)}) fusion(f32[128]{0:T(128)} %copy-done.51, bf16[15,1536]{0,1:T(8,128)(2,1)} %copy-done.5, bf16[128,1536]{0,1:T(8,128)(2,1)S(1)} %copy-done.2, f32[128]{0:T(128)} %copy-done.55, ...), kind=kLoop, calls=%fused_computation.316 | loop fusion | flops 8641536 | bytes 2445312 | tf_op jit(solution)/shard_map/reduce_sum | solution.py:105
  310.6 4.0 collective-permute-start.5
  316.2 2.8 fusion.121
  319.2 2.7 fusion.124
  324.6 2.7 fusion.58
  329.1 2.8 stack.127
  336.0 29.4 %fusion.137 = bf16[128,1536]{0,1:T(8,128)(2,1)S(1)} fusion(f32[128,1536]{0,1:T(8,128)S(1)} %get-tuple-element.82, f32[15,1536]{0,1:T(8,128)} %copy.52, f32[15,1536]{0,1:T(8,128)} %copy.50, f32[128]{0:T(128)} %copy-done.51, f32[1536]{0:T(1024)} %get-tuple-element.80, f32[128]{0:T(128)} %copy-done.52, f32[1536]{0:T(1024)} %get-tuple-element.81, ...), kind=kLoop, calls=%fused_computation.326 | loop fusion | flops 24379392 | bytes 1570304 | tf_op jit(solution)/shard_map/convert_element_type | solution.py:116
  366.4 107.6 %all-reduce.4.cloned.1.call-done = f32[31,1536]{1,0:T(8,128)} async-done(((f32[31,1536]{1,0:T(8,128)}), f32[31,1536]{1,0:T(8,128)}) %all-reduce.4.cloned.1.call-update) | async-done | bytes 190480 | tf_op jit(solution)/shard_map/psum | solution.py:115
  (264 shorter events, 62.7 us)
Async XLA Ops:
  7.2 130.2 %copy-start = (bf16[1,1536,768]{2,1,0:T(8,128)(2,1)S(1)}, bf16[1,1536,768]{2,1,0:T(8,128)(2,1)}, u32[]{:S(2)}) copy-start(bf16[1,1536,768]{2,1,0:T(8,128)(2,1)} %param.14) | copy-start | bytes 7077892
  7.2 37.9 %copy-start.9 = (f32[31,1536]{1,0:T(8,128)S(1)}, f32[31,1536]{1,0:T(8,128)}, u32[]{:S(2)}) copy-start(f32[31,1536]{1,0:T(8,128)} %param.11) | copy-start | bytes 571396
  8.7 39.3 %collective-permute-start.1 = (bf16[15]{0:T(256)(128)(2,1)}, bf16[15]{0:T(256)(128)(2,1)}, u32[]{:S(2)}, u32[]{:S(2)}) collective-permute-start(bf16[15]{0:T(256)(128)(2,1)} %get-tuple-element.122), channel_id=1, source_target_pairs={{0,8},{8,16},{16,24},{24,32},{32,40},{40,48},{48,56},{56,64},{64,7... | collective-permute-start | bytes 98 | tf_op jit(solution)/shard_map/ppermute | solution.py:14
  12.7 35.3 %collective-permute-start.3 = (bf16[15]{0:T(256)(128)(2,1)}, bf16[15]{0:T(256)(128)(2,1)}, u32[]{:S(2)}, u32[]{:S(2)}) collective-permute-start(bf16[15]{0:T(256)(128)(2,1)} %get-tuple-element.123), channel_id=1, source_target_pairs={{8,0},{16,8},{24,16},{32,24},{40,32},{48,40},{56,48},{64,56},{72,6... | collective-permute-start | bytes 98 | tf_op jit(solution)/shard_map/ppermute | solution.py:15
  23.6 56.5 %all-to-all-start.1 = ((bf16[32,1,16]{2,1,0:T(2,128)(2,1)}), bf16[32,1,16]{2,1,0:T(2,128)(2,1)}, u32[]{:S(2)}, u32[]{:S(2)}) async-start(bf16[32,1,16]{2,1,0:T(2,128)(2,1)} %all_to_all.28), calls=%async_computation.1 | async-start | bytes 32768 | tf_op jit(solution)/shard_map/all_to_all | solution.py:65
  38.3 12.5 %collective-permute-start.2 = (bf16[15,1536]{0,1:T(8,128)(2,1)}, bf16[15,1536]{0,1:T(8,128)(2,1)S(1)}, u32[]{:S(2)}, u32[]{:S(2)}) collective-permute-start(bf16[15,1536]{0,1:T(8,128)(2,1)} %copy.45), channel_id=1, source_target_pairs={{8,0},{16,8},{24,16},{32,24},{40,32},{48,40},{56,48},{64,56},{72,6... | collective-permute-start | bytes 138248 | tf_op jit(solution)/shard_map/ppermute | solution.py:15
  40.5 12.1 %collective-permute-start = (bf16[15,1536]{0,1:T(8,128)(2,1)}, bf16[15,1536]{0,1:T(8,128)(2,1)S(1)}, u32[]{:S(2)}, u32[]{:S(2)}) collective-permute-start(bf16[15,1536]{0,1:T(8,128)(2,1)} %copy.43), channel_id=1, source_target_pairs={{0,8},{8,16},{16,24},{24,32},{32,40},{40,48},{48,56},{56,64},{64,7... | collective-permute-start | bytes 138248 | tf_op jit(solution)/shard_map/ppermute | solution.py:14
  48.0 25.0 %copy-start.1 = (bf16[128,1536]{0,1:T(8,128)(2,1)}, bf16[128,1536]{0,1:T(8,128)(2,1)S(1)}, u32[]{:S(2)}) copy-start(bf16[128,1536]{0,1:T(8,128)(2,1)S(1)} %copy.42) | copy-start | bytes 1179652
  50.7 22.2 %copy-start.5 = (bf16[15,1536]{0,1:T(8,128)(2,1)}, bf16[15,1536]{0,1:T(8,128)(2,1)S(1)}, u32[]{:S(2)}) copy-start(bf16[15,1536]{0,1:T(8,128)(2,1)S(1)} %collective-permute-done.2) | copy-start | bytes 138244
  52.6 20.4 %copy-start.3 = (bf16[15,1536]{0,1:T(8,128)(2,1)}, bf16[15,1536]{0,1:T(8,128)(2,1)S(1)}, u32[]{:S(2)}) copy-start(bf16[15,1536]{0,1:T(8,128)(2,1)S(1)} %collective-permute-done) | copy-start | bytes 138244
  80.1 13.8 %copy-start.7 = (bf16[128,1536]{1,0:T(8,128)(2,1)S(1)}, bf16[128,1536]{1,0:T(8,128)(2,1)}, u32[]{:S(2)}) copy-start(bf16[128,1536]{1,0:T(8,128)(2,1)} %param.9) | copy-start | bytes 1179652
  80.1 50.6 %all-to-all-start.2 = ((bf16[32,16,1536]{2,1,0:T(8,128)(2,1)}), bf16[32,16,1536]{2,1,0:T(8,128)(2,1)}, u32[]{:S(2)}, u32[]{:S(2)}) async-start(bf16[32,16,1536]{2,1,0:T(8,128)(2,1)} %bitcast.54), calls=%async_computation.2 | async-start | bytes 3145728 | tf_op jit(solution)/shard_map/all_to_all | solution.py:63
  130.6 42.3 %all-to-all-start = ((bf16[32,16,1536]{2,1,0:T(8,128)(2,1)}), bf16[32,16,1536]{2,1,0:T(8,128)(2,1)}, u32[]{:S(2)}, u32[]{:S(2)}) async-start(bf16[32,16,1536]{2,1,0:T(8,128)(2,1)} %bitcast.55), calls=%async_computation | async-start | bytes 3145728 | tf_op jit(solution)/shard_map/all_to_all | solution.py:64
  136.5 113.7 %reduce-scatter.4.cloned.1.call-start = ((), (), s32[]{:S(2)}) async-start(), calls=%async_computation.7 | async-start | bytes 1769472
  220.7 26.8 %copy-start.73 = (s32[256,1]{0,1:T(1,128)S(1)}, s32[256,1]{0,1:T(1,128)}, u32[]{:S(2)}) copy-start(s32[256,1]{0,1:T(1,128)} %copy-done.72) | copy-start | bytes 3076
  220.7 26.9 %copy-start.8 = (bf16[128,1536]{1,0:T(8,128)(2,1)S(1)}, bf16[128,1536]{1,0:T(8,128)(2,1)}, u32[]{:S(2)}) copy-start(bf16[128,1536]{1,0:T(8,128)(2,1)} %param.9) | copy-start | bytes 1179652
  241.7 15.6 %all-to-all-start.4 = ((f32[32,1,16]{2,1,0:T(1,128)}), f32[32,1,16]{2,1,0:T(1,128)S(1)}, u32[]{:S(2)}, u32[]{:S(2)}) async-start(f32[32,1,16]{2,1,0:T(1,128)} %bitcast.14), calls=%async_computation.4 | async-start | bytes 32768 | tf_op jit(solution)/shard_map/all_to_all | solution.py:93
  257.3 26.3 %all-to-all-start.3 = ((f32[32,16,192]{2,1,0:T(8,128)}), f32[32,16,192]{2,1,0:T(8,128)S(1)}, u32[]{:S(2)}, u32[]{:S(2)}) async-start(f32[32,16,192]{2,1,0:T(8,128)} %convert_element_type.377), calls=%async_computation.3 | async-start | bytes 1048576 | tf_op jit(solution)/shard_map/all_to_all | solution.py:92
  266.2 207.8 %all-reduce.4.cloned.1.call-start = ((), (), s32[]{:S(2)}) async-start(), calls=%async_computation.6 | async-start | bytes 393216 | tf_op jit(solution)/shard_map/psum | solution.py:115
  284.5 15.2 %copy-start.2 = (bf16[128,1536]{0,1:T(8,128)(2,1)S(1)}, bf16[128,1536]{0,1:T(8,128)(2,1)}, u32[]{:S(2)}) copy-start(bf16[128,1536]{0,1:T(8,128)(2,1)} %copy-done.1) | copy-start | bytes 1179652
  310.5 8.6 %copy-start.65 = (f32[128]{0:T(128)S(1)}, f32[128]{0:T(128)}, u32[]{:S(2)}) copy-start(f32[128]{0:T(128)} %copy-done.64) | copy-start | bytes 1540
  310.5 8.6 %copy-start.67 = (f32[128]{0:T(128)S(1)}, f32[128]{0:T(128)}, u32[]{:S(2)}) copy-start(f32[128]{0:T(128)} %copy-done.66) | copy-start | bytes 1540
  310.5 8.6 %copy-start.69 = (f32[128]{0:T(128)S(1)}, f32[128]{0:T(128)}, u32[]{:S(2)}) copy-start(f32[128]{0:T(128)} %copy-done.68) | copy-start | bytes 1540
  310.5 11.3 %copy-start.4 = (bf16[15,1536]{0,1:T(8,128)(2,1)S(1)}, bf16[15,1536]{0,1:T(8,128)(2,1)}, u32[]{:S(2)}) copy-start(bf16[15,1536]{0,1:T(8,128)(2,1)} %copy-done.3) | copy-start | bytes 138244
  310.6 11.3 %copy-start.26 = (f32[128]{0:T(128)S(1)}, f32[128]{0:T(128)}, u32[]{:S(2)}) copy-start(f32[128]{0:T(128)} %copy-done.25) | copy-start | bytes 1540
  310.6 11.3 %copy-start.28 = (f32[128]{0:T(128)S(1)}, f32[128]{0:T(128)}, u32[]{:S(2)}) copy-start(f32[128]{0:T(128)} %copy-done.27) | copy-start | bytes 1540
  310.6 11.3 %copy-start.30 = (f32[128]{0:T(128)S(1)}, f32[128]{0:T(128)}, u32[]{:S(2)}) copy-start(f32[128]{0:T(128)} %copy-done.29) | copy-start | bytes 1540
  310.6 11.3 %copy-start.32 = (f32[128]{0:T(128)S(1)}, f32[128]{0:T(128)}, u32[]{:S(2)}) copy-start(f32[128]{0:T(128)} %copy-done.31) | copy-start | bytes 1540
  310.6 11.3 %copy-start.34 = (f32[128]{0:T(128)S(1)}, f32[128]{0:T(128)}, u32[]{:S(2)}) copy-start(f32[128]{0:T(128)} %copy-done.33) | copy-start | bytes 1540
  310.6 11.3 %copy-start.36 = (f32[128]{0:T(128)S(1)}, f32[128]{0:T(128)}, u32[]{:S(2)}) copy-start(f32[128]{0:T(128)} %copy-done.35) | copy-start | bytes 1540
  310.6 23.3 %collective-permute-start.5 = (f32[15,1536]{1,0:T(8,128)}, f32[15,1536]{1,0:T(8,128)}, u32[]{:S(2)}, u32[]{:S(2)}) collective-permute-start(f32[15,1536]{1,0:T(8,128)} %copy.51), channel_id=1, source_target_pairs={{0,8},{8,16},{16,24},{24,32},{32,40},{40,48},{48,56},{56,64},{64,7... | collective-permute-start | bytes 276488 | tf_op jit(solution)/shard_map/ppermute | solution.py:14
  314.7 17.2 %collective-permute-start.4 = (f32[15,1536]{1,0:T(8,128)}, f32[15,1536]{1,0:T(8,128)}, u32[]{:S(2)}, u32[]{:S(2)}) collective-permute-start(f32[15,1536]{1,0:T(8,128)} %copy.49), channel_id=1, source_target_pairs={{8,0},{16,8},{24,16},{32,24},{40,32},{48,40},{56,48},{64,56},{72,6... | collective-permute-start | bytes 276488 | tf_op jit(solution)/shard_map/ppermute | solution.py:15
  (57 other events, 207.7 us)
Sparse Core Ops, SparseCore 0:
  220.9 29.2 reduce-scatter.3
  332.0 142.0 all-reduce.3
where the time goes:
time: 492 us; the launch traced here: 483 us
  waiting for transfers between devices  179 us (36%)
  local copies, waits for them, and re-layouts  98.5 us (20%)
  other arithmetic  69.8 us (14%)
  starting transfers between devices  64.2 us (13%)
  blocking collectives  35.4 us (7%)
  matrix products  19.9 us (4%)
  between operations  16.1 us (3%)
    psum x1, waiting for transfers between devices, on_device(): kernel_grad = lax.psum(jnp.stack(kernel_rows, 0), 'expert')  108 us
    unnamed x163, local copies, waits for them, and re-layouts  53.3 us
    all_to_all x1, waiting for transfers between devices, on_device(): lax.all_to_all(grad_blocks, 'expert', split_axis=0, concat_axis=0, tiled=...  31.6 us
    all_to_all x1, waiting for transfers between devices, on_device(): lax.all_to_all(mixed_blocks, 'expert', split_axis=0, concat_axis=0, tiled...  31 us
    convert_element_type x1, other arithmetic, on_device(): frames_grad = (mixed_grad + transposed).astype(jnp.bfloat16)  29.4 us
    psum x1, blocking collectives, on_device(): gate_total = lax.psum(gate_part.reshape(n_expert, capacity), 'tensor')  20.8 us
    reduce_sum x6, other arithmetic, on_device(): jnp.sum(mixed_grad * frame_edge[j:j + count].astype(jnp.float32) * masks[...  17.3 us
    convert_element_type x1, other arithmetic, on_device(): mixed = (inputs + conv).astype(jnp.bfloat16)  15.9 us
  transfers between devices with their start and end apart: 13, of which 7 were waited for; matrix products, arithmetic and copies ran while one was open for 26% of the time, Pallas kernels for 0%

commit v1 on v0

v1 whole, which is shorter than its diff:
```python
import jax
import jax.numpy as jnp
from jax import lax
from jax.experimental import pallas as pl
from jax.experimental.pallas import tpu as pltpu
from jax.sharding import PartitionSpec as P

MESH = pl.DeviceIdType.MESH
F32 = jnp.float32
BF16 = jnp.bfloat16
NZ, NY, NX = 8, 4, 4
NE = NZ * NY
F = 128
D = 1536
HS = 768
KW = 31
CAP = 16
SLOTS = NE * CAP
DX = D // NX
NQ = DX // 128
EXT = F + 32


def full_ds(start, size):
    return pl.ds(pl.multiple_of(start, 128), size)


def body(
    frames, cot, seg, kern, ids, gates, w_in, w_out,
    fg_out, kg_out, wig_out, wog_out, gg_out,
    win, wout, wig, wog, rows, sendbuf, src, hs, hr, fx, sx, gsend, grecv, wcol,
    scaled, hidden, pgrad, gacc, gpsend, gpret, ip, sibrecv, cs, r1, s2, r2, fin, ret,
    pmg, pmr, mgx, fgall, kg, krecv, kred, kall, kfull, gg, posr, posc,
    lsem, hsem, asend, arecv, gsem, xsend, ssend, fl, fr, fo, fs, gpsem, sibsem, rsem,
    retsem, pmsem, mhsem, fgsem, ksem, kfsem, ggsem,
):
    e = lax.axis_index("expert")
    t = lax.axis_index("tensor")
    z, y = lax.div(e, NY), lax.rem(e, NY)
    x, c = lax.div(t, 2), lax.rem(t, 2)
    sib = t + 1 - 2 * c
    xr, xl, xo = lax.rem(x + 1, NX), lax.rem(x + 3, NX), lax.rem(x + 2, NX)
    right, left = xr * 2 + c, xl * 2 + c
    xcols = full_ds(x * DX, DX)

    def offset(i):
        p, dy = lax.div(i, NY), lax.rem(i, NY)
        odd = lax.rem(p, 2)
        dz = odd * lax.div(p + 1, 2) + (1 - odd) * lax.rem(NZ - lax.div(p, 2), NZ)
        return dz, dy

    def ahead(i):
        dz, dy = offset(i)
        return lax.rem(z + dz, NZ) * NY + lax.rem(y + dy, NY)

    def behind(i):
        dz, dy = offset(i)
        return lax.rem(z + NZ - dz, NZ) * NY + lax.rem(y + NY - dy, NY)

    def remote(s, d, ss, rs, ee, tt):
        return pltpu.make_async_remote_copy(
            src_ref=s, dst_ref=d, send_sem=ss, recv_sem=rs, device_id=(ee, tt), device_id_type=MESH
        )

    def wait_recv(ref, sem):
        remote(ref, ref, sem, sem, e, sib).wait_recv()

    def wait_send(ref, sem):
        remote(ref, ref, sem, sem, e, sib).wait_send()

    barrier = pltpu.get_barrier_semaphore()

    @pl.loop(1, NE)
    def _(i):
        pl.semaphore_signal(barrier, inc=1, device_id=(ahead(i), t), device_id_type=MESH)

    @pl.loop(1, 2 * NX)
    def _(i):
        pl.semaphore_signal(
            barrier, inc=1, device_id=(e, lax.rem(t + i, 2 * NX)), device_id_type=MESH
        )

    load_in = pltpu.make_async_copy(w_in, win, lsem.at[0])
    load_out = pltpu.make_async_copy(w_out, wout, lsem.at[1])
    load_in.start()
    load_out.start()

    lane = lax.broadcasted_iota(jnp.int32, (F, F), 1)
    sub = lax.broadcasted_iota(jnp.int32, (F, F), 0)
    eye = lane == sub
    idr = [jnp.broadcast_to(ids[k : k + 1, :], (F, F)).astype(F32) for k in range(2)]
    idc = [v.T for v in idr]

    def place(idf, rank):
        idv = idf.astype(jnp.int32)
        dz = (idv // NY - z + NZ) & (NZ - 1)
        dy = (idv - (idv // NY) * NY - y + NY) & (NY - 1)
        p = jnp.maximum(jnp.where(dz <= NZ // 2, 2 * dz - 1, 2 * NZ - 2 * dz), 0)
        return (p * NY + dy) * CAP + rank.astype(jnp.int32)

    for k in range(2):
        hits = jnp.where(idc[0] == idr[k], 1.0, 0.0) + jnp.where(idc[1] == idr[k], 1.0, 0.0)
        rank = jnp.sum(jnp.where(sub < lane, hits, 0.0), axis=0, keepdims=True)
        posr[k] = place(idr[k], jnp.broadcast_to(rank, (F, F)))
        hits = jnp.where(idr[0] == idc[k], 1.0, 0.0) + jnp.where(idr[1] == idc[k], 1.0, 0.0)
        rank = jnp.sum(jnp.where(lane < sub, hits, 0.0), axis=1, keepdims=True)
        posc[k] = place(idc[k], jnp.broadcast_to(rank, (F, F)))

    for g in range(4):
        total = jnp.zeros((1, F), F32)
        for k in range(2):
            gcol = jnp.broadcast_to(gates[k : k + 1, :].astype(F32), (F, F)).T
            total += jnp.sum(
                jnp.where(posc[k] == lane + g * F, gcol, 0.0), axis=0, keepdims=True
            )
        gsend[g] = total
    grecv[0] = gsend[0]

    segr = jnp.broadcast_to(seg[...], (F, F)).astype(F32)
    segc = segr.T
    sx[16 : 16 + F, :] = segc
    hs[0, :, 0:DX] = frames[0:16, xcols]
    hs[1, :, 0:DX] = frames[F - 16 : F, xcols]
    hs[0, :, DX : DX + 128] = segc[0:16].astype(BF16)
    hs[1, :, DX : DX + 128] = segc[F - 16 : F].astype(BF16)

    @pl.loop(0, NQ)
    def _(q):
        fx[16 : 16 + F, full_ds(q * 128, 128)] = frames[:, full_ds(x * DX + q * 128, 128)].astype(
            F32
        )

    pl.semaphore_wait(barrier, NE - 1 + 2 * NX - 1)

    before, after = lax.rem(e + NE - 1, NE), lax.rem(e + 1, NE)
    halo_up = remote(hs.at[1], hr.at[0], hsem.at[0], hsem.at[1], after, t)
    halo_down = remote(hs.at[0], hr.at[1], hsem.at[2], hsem.at[3], before, t)
    halo_up.start()
    halo_down.start()

    def take_halo():
        halo_up.wait_recv()
        halo_down.wait_recv()
        for q in range(NQ):
            fx[0:16, 128 * q : 128 * q + 128] = hr[0, :, 128 * q : 128 * q + 128].astype(F32)
            fx[16 + F : EXT, 128 * q : 128 * q + 128] = hr[1, :, 128 * q : 128 * q + 128].astype(
                F32
            )
        sx[0:16, :] = jnp.where(e == 0, -1.0, hr[0, :, DX : DX + 128].astype(F32))
        sx[16 + F : EXT, :] = jnp.where(e == NE - 1, -1.0, hr[1, :, DX : DX + 128].astype(F32))

    def conv(ext, q, backwards):
        cols = full_ds(q * 128, 128)
        kcols = full_ds(x * DX + q * 128, 128)
        acc = jnp.zeros((F, 128), F32)
        own = sx[16 : 16 + F, :]
        for j in range(KW):
            tap = kern[KW - 1 - j if backwards else j, kcols].reshape(1, 128)
            acc += jnp.where(sx[j + 1 : j + 1 + F, :] == own, ext[j + 1 : j + 1 + F, cols] * tap, 0.0)
        return acc + ext[16 : 16 + F, cols]

    @pl.when(c == 0)
    def _():
        take_halo()

        @pl.loop(0, NQ)
        def _(q):
            src[:, full_ds(q * 128, 128)] = conv(fx, q, False).astype(BF16)

    @pl.when(c == 1)
    def _():
        src[...] = cot[:, xcols]

    @pl.loop(0, 4)
    def _(g):
        slot = sub + g * F
        onehot = jnp.where((posr[0] == slot) | (posr[1] == slot), 1.0, 0.0).astype(BF16)
        gr = full_ds(g * F, F)
        sendbuf[gr, :] = jnp.dot(onehot, src[...], preferred_element_type=F32).astype(BF16)

        @pl.loop(0, 8)
        def _(q):
            i = g * 8 + q
            blk = pl.ds(pl.multiple_of(i * CAP, CAP), CAP)

            @pl.when(i > 0)
            def _():
                to = ahead(i)
                remote(
                    sendbuf.at[blk, :], rows.at[c, blk, xcols], asend.at[0], arecv.at[g], to, t
                ).start()
                remote(gsend.at[g], grecv.at[i], asend.at[1], gsem.at[0], to, t).start()

    rows[c, 0:CAP, xcols] = sendbuf[0:CAP, :]

    @pl.when(c == 1)
    def _():
        take_halo()

    def region(g, xs):
        return rows.at[c, g * F : g * F + F, full_ds(xs * DX, DX)]

    def to_sibling(g, xs):
        r = region(g, xs)
        remote(r, r, ssend.at[0], fs.at[g], e, sib).start()

    def spread(g):
        if g == 0:
            wait_recv(rows.at[c, CAP:F, xcols], arecv.at[0])
        else:
            wait_recv(region(g, x), arecv.at[g])
        r = region(g, x)
        remote(r, r, xsend.at[0], fl.at[g], e, right).start()
        remote(r, r, xsend.at[1], fr.at[g], e, left).start()
        to_sibling(g, x)

    def relay(g):
        r = region(g, xl)
        wait_recv(r, fl.at[g])
        if g % 2 == 0:
            remote(r, r, xsend.at[2], fo.at[g], e, right).start()
        to_sibling(g, xl)
        r = region(g, xr)
        wait_recv(r, fr.at[g])
        if g % 2 == 1:
            remote(r, r, xsend.at[2], fo.at[g], e, left).start()
        to_sibling(g, xr)

    def opposite(g):
        wait_recv(region(g, xo), fo.at[g])
        to_sibling(g, xo)

    def from_sibling(g):
        wait_recv(rows.at[1 - c, g * F : g * F + F, :], fs.at[g])

    def weigh(g):
        parts = [jnp.broadcast_to(grecv[8 * g + q], (CAP, F)) for q in range(8)]
        w = jnp.sum(jnp.where(eye, jnp.concatenate(parts, axis=0), 0.0), axis=1, keepdims=True)
        wcol[g * F : g * F + F, :] = jnp.broadcast_to(w, (F, 128))

    def work(h):
        hr_ = slice(256 * h, 256 * h + 256)
        gacc[hr_, :] = jnp.zeros((256, 128), F32)

        @pl.loop(0, HS // 256)
        def _(n):
            cols = full_ds(n * 256, 256)
            pre = jnp.dot(rows[0, hr_, :], win[:, cols], preferred_element_type=F32)
            back = lax.dot_general(
                rows[1, hr_, :], wout[cols, :], (((1,), (1,)), ((), ())), preferred_element_type=F32
            )
            sig = jax.nn.sigmoid(pre)
            hid = (pre * sig).astype(BF16)
            hidden[hr_, cols] = hid
            prod = hid.astype(F32) * back
            gacc[hr_, :] += prod[:, 0:128] + prod[:, 128:256]
            w = wcol[hr_, 0:1]
            pgrad[hr_, cols] = (back * w * (sig * (1.0 + pre * (1.0 - sig)))).astype(BF16)

        for g in (2 * h, 2 * h + 1):
            part = jnp.sum(gacc[g * F : g * F + F, :], axis=1, keepdims=True)
            row = jnp.sum(
                jnp.where(eye, jnp.broadcast_to(part, (F, F)), 0.0), axis=0, keepdims=True
            )
            gpsend[g] = row
            if g == 0:
                gpret[0] = row

        @pl.loop(max(16 * h, 1), 16 * h + 16)
        def _(i):
            g = lax.div(i, 8)
            remote(gpsend.at[g], gpret.at[i], gpsem.at[0], gpsem.at[1], behind(i), t).start()

    def scale(h):
        @pl.loop(0, D // 256)
        def _(n):
            cols = full_ds(n * 256, 256)
            rh = slice(256 * h, 256 * h + 256)
            scaled[rh, cols] = (wcol[rh, 0:1] * rows[1, rh, cols].astype(F32)).astype(BF16)

    def inputs_grad(h):
        rh = slice(256 * h, 256 * h + 256)

        @pl.loop(0, 3)
        def _(n):
            cols = full_ds(n * 512, 512)
            ip[rh, cols] = lax.dot_general(
                pgrad[rh, :], win[cols, :], (((1,), (1,)), ((), ())), preferred_element_type=F32
            ).astype(BF16)

        other = full_ds((2 * h + 1 - c) * F, F)
        remote(ip.at[other, :], sibrecv.at[h], sibsem.at[0], sibsem.at[1 + h], e, sib).start()

    def ring1(h):
        wait_recv(sibrecv.at[h], sibsem.at[1 + h])
        own = full_ds((2 * h + c) * F, F)
        cs[h] = (ip[own, :].astype(F32) + sibrecv[h].astype(F32)).astype(BF16)
        oc = full_ds(xo * DX, DX)
        remote(cs.at[h, 0:64, oc], r1.at[h, 0], rsem.at[0], rsem.at[2 + h], e, right).start()
        remote(cs.at[h, 64:128, oc], r1.at[h, 1], rsem.at[1], rsem.at[4 + h], e, left).start()

    def ring2(h):
        wait_recv(r1.at[h, 0], rsem.at[2 + h])
        rc = full_ds(xr * DX, DX)
        s2[h, 0, 0:64, :] = (cs[h, 0:64, rc].astype(F32) + r1[h, 0].astype(F32)).astype(BF16)
        s2[h, 0, 64:128, :] = cs[h, 64:128, rc]
        remote(s2.at[h, 0], r2.at[h, 0], rsem.at[6], rsem.at[8 + h], e, right).start()
        wait_recv(r1.at[h, 1], rsem.at[4 + h])
        lc = full_ds(xl * DX, DX)
        s2[h, 1, 64:128, :] = (cs[h, 64:128, lc].astype(F32) + r1[h, 1].astype(F32)).astype(BF16)
        s2[h, 1, 0:64, :] = cs[h, 0:64, lc]
        remote(s2.at[h, 1], r2.at[h, 1], rsem.at[7], rsem.at[10 + h], e, left).start()

    def ring3(h):
        wait_recv(r2.at[h, 0], rsem.at[8 + h])
        wait_recv(r2.at[h, 1], rsem.at[10 + h])
        fin[h] = (
            cs[h, :, xcols].astype(F32) + r2[h, 0].astype(F32) + r2[h, 1].astype(F32)
        ).astype(BF16)

        @pl.loop(0, 8)
        def _(q):
            i = (2 * h + c) * 8 + q
            blk = pl.ds(pl.multiple_of(q * CAP, CAP), CAP)

            @pl.when(i > 0)
            def _():
                remote(
                    fin.at[h, blk, :], ret.at[h, blk, :], retsem.at[0], retsem.at[1 + h], behind(i), t
                ).start()

        if h == 0:

            @pl.when(c == 0)
            def _():
                ret[0, 0:CAP, :] = fin[0, 0:CAP, :]

    def first_grad(lo, hi):
        @pl.loop(lo, hi)
        def _(m):
            cols = full_ds(m * 256, 256)
            wig[cols, :] = lax.dot_general(
                rows[0, :, cols], pgrad[...], (((0,), (0,)), ((), ())), preferred_element_type=F32
            ).astype(BF16)

    def second_grad(lo, hi):
        @pl.loop(lo, hi)
        def _(m):
            cols = full_ds(m * 256, 256)
            for n in range(2):
                nc = slice(n * 768, n * 768 + 768)
                wog[cols, nc] = lax.dot_general(
                    hidden[:, cols], scaled[:, nc], (((0,), (0,)), ((), ())),
                    preferred_element_type=F32,
                ).astype(BF16)

    spread(0)
    spread(1)
    relay(0)
    spread(2)
    relay(1)
    opposite(0)
    spread(3)
    relay(2)
    opposite(1)
    wait_recv(grecv.at[1:NE], gsem.at[0])
    for g in range(4):
        weigh(g)
    load_in.wait()
    load_out.wait()
    from_sibling(0)
    from_sibling(1)
    work(0)
    relay(3)
    opposite(2)
    inputs_grad(0)
    opposite(3)
    scale(0)
    ring1(0)
    from_sibling(2)
    from_sibling(3)
    work(1)
    ring2(0)
    inputs_grad(1)
    ring3(0)
    scale(1)
    first_grad(0, 2)
    ring1(1)
    first_grad(2, 6)
    ring2(1)
    store_in = pltpu.make_async_copy(wig, wig_out, lsem.at[2])
    store_in.start()
    second_grad(0, 2)
    ring3(1)
    second_grad(2, 3)
    store_out = pltpu.make_async_copy(wog, wog_out, lsem.at[3])
    store_out.start()

    wait_recv(gpret.at[1:NE], gpsem.at[1])
    gcols = [jnp.zeros((F, F), F32) for _ in range(2)]
    for g in range(4):
        row = jnp.zeros((1, F), F32)
        for q in range(8):
            row += jnp.where(lax.div(lane[0:1, :], CAP) == q, gpret[8 * g + q], 0.0)
        row = jnp.broadcast_to(row, (F, F))
        for k in range(2):
            gcols[k] += jnp.where(posc[k] == lane + g * F, row, 0.0)
    for k in range(2):
        col = jnp.sum(gcols[k], axis=1, keepdims=True)
        gg[t, k : k + 1, :] = jnp.sum(
            jnp.where(eye, jnp.broadcast_to(col, (F, F)), 0.0), axis=0, keepdims=True
        )

    @pl.loop(1, 2 * NX)
    def _(i):
        remote(
            gg.at[t], gg.at[t], ggsem.at[0], ggsem.at[1], e, lax.rem(t + i, 2 * NX)
        ).start()

    @pl.when(c == 0)
    def _():
        wait_recv(ret.at[0, CAP:F, :], retsem.at[1])

    @pl.when(c == 1)
    def _():
        wait_recv(ret.at[0], retsem.at[1])

    wait_recv(ret.at[1], retsem.at[2])
    picks = []
    for h in range(2):
        slot = lane + (2 * h + c) * F
        picks.append(
            jnp.where((posc[0] == slot) | (posc[1] == slot), 1.0, 0.0).astype(BF16)
        )
    pmg[...] = jnp.dot(picks[0], ret[0], preferred_element_type=F32) + jnp.dot(
        picks[1], ret[1], preferred_element_type=F32
    )
    swap = remote(pmg, pmr, pmsem.at[0], pmsem.at[1], e, sib)
    swap.start()
    swap.wait_recv()
    mgx[16 : 16 + F, :] = cot[:, xcols].astype(F32) + (pmg[...] + pmr[...])

    @pl.when(c == 0)
    def _():
        up = remote(
            mgx.at[F : F + 16, :], mgx.at[0:16, :], mhsem.at[0], mhsem.at[1], after, t
        )
        down = remote(
            mgx.at[16:32, :], mgx.at[16 + F : EXT, :], mhsem.at[2], mhsem.at[3], before, t
        )
        up.start()
        down.start()
        up.wait_recv()
        down.wait_recv()

        @pl.loop(0, NQ)
        def _(q):
            fgall[:, full_ds(x * DX + q * 128, 128)] = conv(mgx, q, True).astype(BF16)

        @pl.loop(1, 2 * NX)
        def _(i):
            r = fgall.at[:, xcols]
            remote(r, r, fgsem.at[0], fgsem.at[1], e, lax.rem(t + i, 2 * NX)).start()

        wait_recv(fgall.at[:, 0 : 3 * DX], fgsem.at[1])
        wait_recv(kfull, kfsem.at[1])
        wait_send(ip.at[0 : 3 * F, 0:896], fgsem.at[0])
        up.wait_send()
        down.wait_send()

    @pl.when(c == 1)
    def _():
        kg[...] = jnp.zeros_like(kg)

        @pl.loop(0, NQ)
        def _(q):
            cols = full_ds(q * 128, 128)
            own = sx[16 : 16 + F, :]
            mg = mgx[16 : 16 + F, cols]
            for j in range(KW):
                prod = jnp.where(
                    sx[j + 1 : j + 1 + F, :] == own, fx[j + 1 : j + 1 + F, cols] * mg, 0.0
                )
                kg[j, pl.ds(q, 1), :] = jnp.sum(prod, axis=0, keepdims=True)

        krecv[0] = kg[e]

        @pl.loop(1, NE)
        def _(i):
            to = ahead(i)
            remote(kg.at[to], krecv.at[i], ksem.at[0], ksem.at[1], to, t).start()

        wait_recv(krecv.at[1:NE], ksem.at[1])
        kred[...] = jnp.sum(krecv[...], axis=0)
        kall[0] = kred[...]
        korder = kall

        @pl.loop(1, NE)
        def _(i):
            remote(kred, korder.at[i], ksem.at[2], ksem.at[3], ahead(i), t).start()

        wait_recv(kall.at[1:NE], ksem.at[3])

        @pl.loop(0, NE)
        def _(i):
            kfull[x, behind(i)] = kall[i]

        @pl.loop(1, 2 * NX)
        def _(i):
            remote(
                kfull.at[x], kfull.at[x], kfsem.at[0], kfsem.at[1], e, lax.rem(t + i, 2 * NX)
            ).start()

        wait_recv(kfull.at[0:3], kfsem.at[1])
        wait_recv(fgall, fgsem.at[1])
        wait_send(kg.at[1:NE], ksem.at[0])
        wait_send(kg.at[1:NE], ksem.at[2])
        wait_send(ip.at[0 : 2 * F, 0:896], kfsem.at[0])

    wait_recv(gg.at[1 : 2 * NX], ggsem.at[1])
    gg_out[...] = jnp.sum(gg[...], axis=0)
    fg_out[...] = fgall[...]
    for xs in range(NX):
        for q in range(NQ):
            kg_out[:, xs * DX + q * 128 : xs * DX + q * 128 + 128] = kfull[xs, 0:KW, q, :]

    store_in.wait()
    store_out.wait()
    halo_up.wait_send()
    halo_down.wait_send()
    wait_send(sendbuf.at[CAP:SLOTS, :], asend.at[0])
    wait_send(grecv.at[1:NE], asend.at[1])
    wait_send(rows.at[c, :, xcols], xsend.at[0])
    wait_send(rows.at[c, :, xcols], xsend.at[1])
    wait_send(rows.at[c, :, xcols], xsend.at[2])
    wait_send(rows.at[c], ssend.at[0])
    wait_send(gpret.at[1:NE], gpsem.at[0])
    wait_send(sibrecv, sibsem.at[0])
    wait_send(r1.at[:, 0], rsem.at[0])
    wait_send(r1.at[:, 1], rsem.at[1])
    wait_send(s2.at[:, 0], rsem.at[6])
    wait_send(s2.at[:, 1], rsem.at[7])

    @pl.when(c == 0)
    def _():
        wait_send(ip.at[CAP : 2 * F, 0:DX], retsem.at[0])

    @pl.when(c == 1)
    def _():
        wait_send(ip.at[0 : 2 * F, 0:DX], retsem.at[0])

    swap.wait_send()
    wait_send(gg.at[1 : 2 * NX], ggsem.at[0])


def on_device(frames, cotangent, segment_ids, kernel, expert_ids, gates, w_in, w_out):
    vmem = pl.BlockSpec(memory_space=pltpu.VMEM)
    anywhere = pl.BlockSpec(memory_space=pl.ANY)
    dma = pltpu.SemaphoreType.DMA
    V = pltpu.VMEM
    scratch = dict(
        win=V((D, HS), BF16),
        wout=V((HS, D), BF16),
        wig=V((D, HS), BF16),
        wog=V((HS, D), BF16),
        rows=V((2, SLOTS, D), BF16),
        sendbuf=V((SLOTS, DX), BF16),
        src=V((F, DX), BF16),
        hs=V((2, 16, DX + 128), BF16),
        hr=V((2, 16, DX + 128), BF16),
        fx=V((EXT, DX), F32),
        sx=V((EXT, 128), F32),
        gsend=V((4, 1, 128), F32),
        grecv=V((NE, 1, 128), F32),
        wcol=V((SLOTS, 128), F32),
        scaled=V((SLOTS, D), BF16),
        hidden=V((SLOTS, HS), BF16),
        pgrad=V((SLOTS, HS), BF16),
        gacc=V((SLOTS, 128), F32),
        gpsend=V((4, 1, 128), F32),
        gpret=V((NE, 1, 128), F32),
        ip=V((SLOTS, D), BF16),
        sibrecv=V((2, F, D), BF16),
        cs=V((2, F, D), BF16),
        r1=V((2, 2, F // 2, DX), BF16),
        s2=V((2, 2, F, DX), BF16),
        r2=V((2, 2, F, DX), BF16),
        fin=V((2, F, DX), BF16),
        ret=V((2, F, DX), BF16),
        pmg=V((F, DX), F32),
        pmr=V((F, DX), F32),
        mgx=V((EXT, DX), F32),
        fgall=V((F, D), BF16),
        kg=V((NE, 4, 128), F32),
        krecv=V((NE, 4, 128), F32),
        kred=V((4, 128), F32),
        kall=V((NE, 4, 128), F32),
        kfull=V((NX, NE, 4, 128), F32),
        gg=V((2 * NX, 2, 128), F32),
        posr=V((2, F, F), jnp.int32),
        posc=V((2, F, F), jnp.int32),
        lsem=dma((4,)),
        hsem=dma((4,)),
        asend=dma((2,)),
        arecv=dma((4,)),
        gsem=dma((1,)),
        xsend=dma((3,)),
        ssend=dma((1,)),
        fl=dma((4,)),
        fr=dma((4,)),
        fo=dma((4,)),
        fs=dma((4,)),
        gpsem=dma((2,)),
        sibsem=dma((3,)),
        rsem=dma((12,)),
        retsem=dma((3,)),
        pmsem=dma((2,)),
        mhsem=dma((4,)),
        fgsem=dma((2,)),
        ksem=dma((4,)),
        kfsem=dma((2,)),
        ggsem=dma((2,)),
    )
    fg, kg, wig, wog, gg = pl.pallas_call(
        body,
        out_shape=(
            jax.ShapeDtypeStruct((F, D), BF16),
            jax.ShapeDtypeStruct((KW, D), F32),
            jax.ShapeDtypeStruct((D, HS), BF16),
            jax.ShapeDtypeStruct((HS, D), BF16),
            jax.ShapeDtypeStruct((2, F), F32),
        ),
        in_specs=[vmem] * 6 + [anywhere] * 2,
        out_specs=(vmem, vmem, anywhere, anywhere, vmem),
        scratch_shapes=list(scratch.values()),
        compiler_params=pltpu.CompilerParams(
            collective_id=0, has_side_effects=True, vmem_limit_bytes=56 * 1024 * 1024
        ),
    )(
        frames,
        cotangent,
        segment_ids.reshape(1, F),
        kernel,
        expert_ids.T,
        gates.T,
        w_in[0],
        w_out[0],
    )
    return fg, kg, wig[None], wog[None], gg.T


def solution(mesh):
    return jax.shard_map(
        on_device,
        mesh=mesh,
        in_specs=(
            P("expert", None),
            P("expert", None),
            P("expert"),
            P(),
            P("expert", None),
            P("expert", None),
            P("expert", None, "tensor"),
            P("expert", "tensor", None),
        ),
        out_specs=(
            P("expert", None),
            P(),
            P("expert", None, "tensor"),
            P("expert", "tensor", None),
            P("expert", None),
        ),
        check_vma=False,
    )
```

time: 492 us -> 97.2 us (0.20)
  the two profiles are of different devices: /device:TPU:2 before, /device:TPU:1 now
where the time goes in v1:
time: 97.2 us; the launch traced here: 97.1 us
  Pallas kernels  87.7 us (90%)
  local copies, waits for them, and re-layouts  8.73 us (9%)
    pallas_call x1, Pallas kernels, on_device(): pl.pallas_call(body, out_shape=(jax.ShapeDtypeStruct((F, D), BF16), jax.S...  87.7 us
    unnamed x9, local copies, waits for them, and re-layouts  8.73 us

profile of v1, /device:TPU:1, one launch (start us, length us, event | category | flops | bytes accessed | tf_op | source)
XLA Modules:
  0.0 97.1 jit_solution(1419441272225822593)
XLA Ops:
  0.6 87.7 %shard_map.119 = (bf16[128,1536]{1,0:T(8,128)(2,1)}, f32[31,1536]{1,0:T(8,128)}, bf16[1536,768]{1,0:T(8,128)(2,1)}, bf16[768,1536]{1,0:T(8,128)(2,1)}, f32[2,128]{1,0:T(2,128)}) custom-call(bf16[128,1536]{1,0:T(8,128)(2,1)} %frames.1, bf16[128,1536]{1,0:T(8,128)(2,1)} %cot.1, s32[1,128]{1,0:T(1,128)} %bitcast.14, f32[31,1536]{1,0:T(8,128)} %kern.1, ...), custom_call_target="tpu_custom_call" | custom-call | tf_op jit(solution)/shard_map/pallas_call | solution.py:624
  88.3 1.8 %copy.18 = bf16[128,1536]{1,0:T(8,128)(2,1)} copy(bf16[128,1536]{1,0:T(8,128)(2,1)} %get-tuple-element.20) | data formatting | bytes 786432
  90.1 1.6 %copy.19 = f32[31,1536]{1,0:T(8,128)} copy(f32[31,1536]{1,0:T(8,128)} %get-tuple-element.21) | data formatting | bytes 380928
  91.7 0.0 copy-start
  91.7 3.4 %copy.20 = bf16[1,1536,768]{2,1,0:T(8,128)(2,1)} copy(bf16[1,1536,768]{2,1,0:T(8,128)(2,1)} %bitcast.11) | data formatting | bytes 4718592
  95.1 0.0 copy-done
  95.1 0.0 copy-start.1
  95.1 1.4 %copy.21 = bf16[1,768,1536]{2,1,0:T(8,128)(2,1)} copy(bf16[1,768,1536]{2,1,0:T(8,128)(2,1)S(1)} %bitcast.10) | data formatting | bytes 4718592
  96.5 0.0 copy-done.1
  96.5 0.6 copy.22
Async XLA Ops:
  91.7 3.4 %copy-start = (bf16[768,1536]{1,0:T(8,128)(2,1)S(1)}, bf16[768,1536]{1,0:T(8,128)(2,1)}, u32[]{:S(2)}) copy-start(bf16[768,1536]{1,0:T(8,128)(2,1)} %get-tuple-element.13) | copy-start | bytes 7077892
  95.1 1.4 %copy-start.1 = (f32[2,128]{1,0:T(2,128)S(1)}, f32[2,128]{1,0:T(2,128)}, u32[]{:S(2)}) copy-start(f32[2,128]{1,0:T(2,128)} %get-tuple-element.14) | copy-start | bytes 3076

commit v2 on v1

--- a/solution.py
+++ b/solution.py
@@ -26,11 +26,12 @@
 
 
 def body(
-    frames, cot, seg, kern, ids, gates, w_in, w_out,
-    fg_out, kg_out, wig_out, wog_out, gg_out,
-    win, wout, wig, wog, rows, sendbuf, src, hs, hr, fx, sx, gsend, grecv, wcol,
-    scaled, hidden, pgrad, gacc, gpsend, gpret, ip, sibrecv, cs, r1, s2, r2, fin, ret,
-    pmg, pmr, mgx, fgall, kg, krecv, kred, kall, kfull, gg, posr, posc,
+    frames_in, cot_in, seg_in, kern_in, ids_in, gates_in, w_in, w_out,
+    fg_out, kg_out, wig, wog, gg_out,
+    frames, cot, seg, kern, ids, gates,
+    win, wout, rows, sendbuf, src, hs, hr, fx, sx, gsend, grecv, wcol,
+    scaled, hidden, pgrad, gacc, gpsend, gpx, gprow, gpret, ip, sibrecv, cs, r1, s2, r2, fin, ret,
+    pmg, pmr, mgx, fgall, kg, krecv, kred, kfull, gg, posr, posc,
     lsem, hsem, asend, arecv, gsem, xsend, ssend, fl, fr, fo, fs, gpsem, sibsem, rsem,
     retsem, pmsem, mhsem, fgsem, ksem, kfsem, ggsem,
 ):
@@ -40,22 +41,23 @@
     x, c = lax.div(t, 2), lax.rem(t, 2)
     sib = t + 1 - 2 * c
     xr, xl, xo = lax.rem(x + 1, NX), lax.rem(x + 3, NX), lax.rem(x + 2, NX)
-    right, left = xr * 2 + c, xl * 2 + c
+    right, left, facing = xr * 2 + c, xl * 2 + c, xo * 2 + c
     xcols = full_ds(x * DX, DX)
 
+    zt = [lax.rem(z + k, NZ) * NY for k in range(NZ)]
+    yt = [lax.rem(y + k, NY) for k in range(NY)]
+
     def offset(i):
-        p, dy = lax.div(i, NY), lax.rem(i, NY)
-        odd = lax.rem(p, 2)
-        dz = odd * lax.div(p + 1, 2) + (1 - odd) * lax.rem(NZ - lax.div(p, 2), NZ)
-        return dz, dy
+        p = i // NY
+        return ((p + 1) // 2 if p % 2 else (NZ - p // 2) % NZ), i % NY
 
     def ahead(i):
         dz, dy = offset(i)
-        return lax.rem(z + dz, NZ) * NY + lax.rem(y + dy, NY)
+        return zt[dz] + yt[dy]
 
     def behind(i):
         dz, dy = offset(i)
-        return lax.rem(z + NZ - dz, NZ) * NY + lax.rem(y + NY - dy, NY)
+        return zt[(NZ - dz) % NZ] + yt[(NY - dy) % NY]
 
     def remote(s, d, ss, rs, ee, tt):
         return pltpu.make_async_remote_copy(
@@ -70,20 +72,21 @@
 
     barrier = pltpu.get_barrier_semaphore()
 
-    @pl.loop(1, NE)
-    def _(i):
+    for i in range(1, NE):
         pl.semaphore_signal(barrier, inc=1, device_id=(ahead(i), t), device_id_type=MESH)
-
-    @pl.loop(1, 2 * NX)
-    def _(i):
+    for i in range(1, 2 * NX):
         pl.semaphore_signal(
             barrier, inc=1, device_id=(e, lax.rem(t + i, 2 * NX)), device_id_type=MESH
         )
-
-    load_in = pltpu.make_async_copy(w_in, win, lsem.at[0])
-    load_out = pltpu.make_async_copy(w_out, wout, lsem.at[1])
-    load_in.start()
-    load_out.start()
+    pairs = (
+        (ids_in, ids), (gates_in, gates), (seg_in, seg), (frames_in, frames), (cot_in, cot),
+        (kern_in, kern), (w_in, win), (w_out, wout),
+    )
+    loads = [pltpu.make_async_copy(a, b, lsem.at[k]) for k, (a, b) in enumerate(pairs)]
+    for load in loads:
+        load.start()
+    for load in loads[:3]:
+        load.wait()
 
     lane = lax.broadcasted_iota(jnp.int32, (F, F), 1)
     sub = lax.broadcasted_iota(jnp.int32, (F, F), 0)
@@ -114,8 +117,13 @@
                 jnp.where(posc[k] == lane + g * F, gcol, 0.0), axis=0, keepdims=True
             )
         gsend[g] = total
-    grecv[0] = gsend[0]
-
+
+    @pl.when(c == 1)
+    def _():
+        grecv[0] = gsend[0]
+
+    for load in loads[3:6]:
+        load.wait()
     segr = jnp.broadcast_to(seg[...], (F, F)).astype(F32)
     segc = segr.T
     sx[16 : 16 + F, :] = segc
@@ -171,27 +179,28 @@
     def _():
         src[...] = cot[:, xcols]
 
-    @pl.loop(0, 4)
-    def _(g):
+    def issue(g):
         slot = sub + g * F
         onehot = jnp.where((posr[0] == slot) | (posr[1] == slot), 1.0, 0.0).astype(BF16)
-        gr = full_ds(g * F, F)
+        gr = slice(g * F, g * F + F)
         sendbuf[gr, :] = jnp.dot(onehot, src[...], preferred_element_type=F32).astype(BF16)
-
-        @pl.loop(0, 8)
-        def _(q):
-            i = g * 8 + q
-            blk = pl.ds(pl.multiple_of(i * CAP, CAP), CAP)
-
-            @pl.when(i > 0)
-            def _():
-                to = ahead(i)
-                remote(
-                    sendbuf.at[blk, :], rows.at[c, blk, xcols], asend.at[0], arecv.at[g], to, t
-                ).start()
-                remote(gsend.at[g], grecv.at[i], asend.at[1], gsem.at[0], to, t).start()
-
-    rows[c, 0:CAP, xcols] = sendbuf[0:CAP, :]
+        for i in range(max(8 * g, 1), 8 * g + 8):
+            blk = slice(i * CAP, i * CAP + CAP)
+            remote(
+                sendbuf.at[blk, :], rows.at[c, blk, xcols], asend.at[0], arecv.at[g], ahead(i), t
+            ).start()
+        if g == 0:
+            rows[c, 0:CAP, xcols] = sendbuf[0:CAP, :]
+
+    issue(0)
+    issue(1)
+
+    @pl.when(c == 1)
+    def _():
+        for i in range(1, NE):
+            remote(
+                gsend.at[i // 8], grecv.at[i], asend.at[1], gsem.at[0], ahead(i), t
+            ).start()
 
     @pl.when(c == 1)
     def _():
@@ -217,13 +226,13 @@
     def relay(g):
         r = region(g, xl)
         wait_recv(r, fl.at[g])
-        if g % 2 == 0:
-            remote(r, r, xsend.at[2], fo.at[g], e, right).start()
+        lo = rows.at[c, g * F : g * F + F // 2, full_ds(xl * DX, DX)]
+        remote(lo, lo, xsend.at[2], fo.at[g], e, right).start()
         to_sibling(g, xl)
         r = region(g, xr)
         wait_recv(r, fr.at[g])
-        if g % 2 == 1:
-            remote(r, r, xsend.at[2], fo.at[g], e, left).start()
+        hi = rows.at[c, g * F + F // 2 : g * F + F, full_ds(xr * DX, DX)]
+        remote(hi, hi, xsend.at[2], fo.at[g], e, left).start()
         to_sibling(g, xr)
 
     def opposite(g):
@@ -263,13 +272,61 @@
                 jnp.where(eye, jnp.broadcast_to(part, (F, F)), 0.0), axis=0, keepdims=True
             )
             gpsend[g] = row
-            if g == 0:
-                gpret[0] = row
-
-        @pl.loop(max(16 * h, 1), 16 * h + 16)
-        def _(i):
-            g = lax.div(i, 8)
-            remote(gpsend.at[g], gpret.at[i], gpsem.at[0], gpsem.at[1], behind(i), t).start()
+
+        for tt in range(4 * h, 4 * h + 4):
+
+            @pl.when(t == tt)
+            def _():
+                gpx[tt] = gpsend[tt // 2]
+
+            @pl.when(t != tt)
+            def _():
+                remote(
+                    gpsend.at[tt // 2], gpx.at[t], gpsem.at[0], gpsem.at[1], e, tt
+                ).start()
+
+    def gates_on():
+        wait_recv(gpx.at[1 : 2 * NX], gpsem.at[1])
+        gprow[0] = jnp.sum(gpx[...], axis=0)
+        dz = c * (x + 1) + (1 - c) * lax.rem(NZ - x, NZ)
+        zz = lax.rem(z + NZ - dz, NZ) * NY
+
+        @pl.when(t == 0)
+        def _():
+            gpret[0] = gprow[0]
+
+        @pl.when(t > 0)
+        def _():
+            remote(gprow.at[0], gpret.at[0], gpsem.at[2], gpsem.at[3], zz + yt[0], t).start()
+
+        for j in range(1, NY):
+            remote(
+                gprow.at[0], gpret.at[j], gpsem.at[2], gpsem.at[3], zz + yt[NY - j], t
+            ).start()
+
+    def gates_home():
+        @pl.when(t == 0)
+        def _():
+            wait_recv(gpret.at[1:NY], gpsem.at[3])
+
+        @pl.when(t > 0)
+        def _():
+            wait_recv(gpret, gpsem.at[3])
+
+        row = jnp.zeros((1, F), F32)
+        for j in range(NY):
+            row += jnp.where(lax.div(lane[0:1, :], CAP) == 4 * c + j, gpret[j], 0.0)
+        row = jnp.broadcast_to(row, (F, F))
+        for k in range(2):
+            hit = jnp.where(posc[k] == lane + x * F, row, 0.0)
+            col = jnp.sum(hit, axis=1, keepdims=True)
+            gg[t, k : k + 1, :] = jnp.sum(
+                jnp.where(eye, jnp.broadcast_to(col, (F, F)), 0.0), axis=0, keepdims=True
+            )
+        for i in range(1, 2 * NX):
+            remote(
+                gg.at[t], gg.at[t], ggsem.at[0], ggsem.at[1], e, lax.rem(t + i, 2 * NX)
+            ).start()
 
     def scale(h):
         @pl.loop(0, D // 256)
@@ -318,22 +375,25 @@
             cs[h, :, xcols].astype(F32) + r2[h, 0].astype(F32) + r2[h, 1].astype(F32)
         ).astype(BF16)
 
-        @pl.loop(0, 8)
-        def _(q):
-            i = (2 * h + c) * 8 + q
-            blk = pl.ds(pl.multiple_of(q * CAP, CAP), CAP)
-
-            @pl.when(i > 0)
-            def _():
+        for q in range(8):
+            blk = slice(q * CAP, q * CAP + CAP)
+            i = 16 * h + q
+
+            def send():
+                to = jnp.where(c == 0, behind(i), behind(i + 8))
                 remote(
-                    fin.at[h, blk, :], ret.at[h, blk, :], retsem.at[0], retsem.at[1 + h], behind(i), t
+                    fin.at[h, blk, :], ret.at[h, blk, :], retsem.at[0], retsem.at[1 + h], to, t
                 ).start()
 
-        if h == 0:
-
-            @pl.when(c == 0)
-            def _():
-                ret[0, 0:CAP, :] = fin[0, 0:CAP, :]
+            if i == 0:
+
+                @pl.when(c == 0)
+                def _():
+                    ret[0, 0:CAP, :] = fin[0, 0:CAP, :]
+
+                pl.when(c == 1)(send)
+            else:
+                send()
 
     def first_grad(lo, hi):
         @pl.loop(lo, hi)
@@ -355,19 +415,33 @@
                 ).astype(BF16)
 
     spread(0)
+    issue(2)
     spread(1)
     relay(0)
+    issue(3)
     spread(2)
     relay(1)
     opposite(0)
+
+    share = remote(grecv, grecv, gsem.at[1], gsem.at[2], e, sib)
+
+    @pl.when(c == 1)
+    def _():
+        wait_recv(grecv.at[1:NE], gsem.at[0])
+        share.start()
+
     spread(3)
     relay(2)
     opposite(1)
-    wait_recv(grecv.at[1:NE], gsem.at[0])
+
+    @pl.when(c == 0)
+    def _():
+        share.wait_recv()
+
     for g in range(4):
         weigh(g)
-    load_in.wait()
-    load_out.wait()
+    for load in loads[6:]:
+        load.wait()
     from_sibling(0)
     from_sibling(1)
     work(0)
@@ -386,36 +460,13 @@
     scale(1)
     first_grad(0, 2)
     ring1(1)
-    first_grad(2, 6)
+    gates_on()
+    first_grad(2, 5)
     ring2(1)
-    store_in = pltpu.make_async_copy(wig, wig_out, lsem.at[2])
-    store_in.start()
+    first_grad(5, 6)
     second_grad(0, 2)
     ring3(1)
     second_grad(2, 3)
-    store_out = pltpu.make_async_copy(wog, wog_out, lsem.at[3])
-    store_out.start()
-
-    wait_recv(gpret.at[1:NE], gpsem.at[1])
-    gcols = [jnp.zeros((F, F), F32) for _ in range(2)]
-    for g in range(4):
-        row = jnp.zeros((1, F), F32)
-        for q in range(8):
-            row += jnp.where(lax.div(lane[0:1, :], CAP) == q, gpret[8 * g + q], 0.0)
-        row = jnp.broadcast_to(row, (F, F))
-        for k in range(2):
-            gcols[k] += jnp.where(posc[k] == lane + g * F, row, 0.0)
-    for k in range(2):
-        col = jnp.sum(gcols[k], axis=1, keepdims=True)
-        gg[t, k : k + 1, :] = jnp.sum(
-            jnp.where(eye, jnp.broadcast_to(col, (F, F)), 0.0), axis=0, keepdims=True
-        )
-
-    @pl.loop(1, 2 * NX)
-    def _(i):
-        remote(
-            gg.at[t], gg.at[t], ggsem.at[0], ggsem.at[1], e, lax.rem(t + i, 2 * NX)
-        ).start()
 
     @pl.when(c == 0)
     def _():
@@ -437,8 +488,21 @@
     )
     swap = remote(pmg, pmr, pmsem.at[0], pmsem.at[1], e, sib)
     swap.start()
+    gates_home()
     swap.wait_recv()
     mgx[16 : 16 + F, :] = cot[:, xcols].astype(F32) + (pmg[...] + pmr[...])
+
+    def gather_own(r, sem):
+        remote(r, r, sem.at[0], sem.at[3], e, facing).start()
+        remote(r, r, sem.at[0], sem.at[1], e, right).start()
+        remote(r, r, sem.at[0], sem.at[2], e, left).start()
+        remote(r, r, sem.at[4], sem.at[5], e, sib).start()
+
+    def gather_rest(view, sem):
+        for k, xs in ((1, xl), (2, xr), (3, xo)):
+            r = view(xs)
+            wait_recv(r, sem.at[k])
+            remote(r, r, sem.at[4], sem.at[5], e, sib).start()
 
     @pl.when(c == 0)
     def _():
@@ -453,69 +517,51 @@
         up.wait_recv()
         down.wait_recv()
 
-        @pl.loop(0, NQ)
-        def _(q):
-            fgall[:, full_ds(x * DX + q * 128, 128)] = conv(mgx, q, True).astype(BF16)
-
-        @pl.loop(1, 2 * NX)
-        def _(i):
-            r = fgall.at[:, xcols]
-            remote(r, r, fgsem.at[0], fgsem.at[1], e, lax.rem(t + i, 2 * NX)).start()
-
-        wait_recv(fgall.at[:, 0 : 3 * DX], fgsem.at[1])
-        wait_recv(kfull, kfsem.at[1])
-        wait_send(ip.at[0 : 3 * F, 0:896], fgsem.at[0])
+        for q in range(NQ):
+            tile = full_ds(x * DX + q * 128, 128)
+            fgall[:, tile] = conv(mgx, q, True).astype(BF16)
+            gather_own(fgall.at[:, tile], fgsem)
+        gather_rest(lambda xs: fgall.at[:, full_ds(xs * DX, DX)], fgsem)
+        wait_recv(kfull, kfsem.at[5])
+        wait_send(fgall.at[:, 0 : 3 * DX], fgsem.at[0])
+        wait_send(fgall, fgsem.at[4])
         up.wait_send()
         down.wait_send()
 
     @pl.when(c == 1)
     def _():
         kg[...] = jnp.zeros_like(kg)
-
-        @pl.loop(0, NQ)
-        def _(q):
-            cols = full_ds(q * 128, 128)
-            own = sx[16 : 16 + F, :]
-            mg = mgx[16 : 16 + F, cols]
-            for j in range(KW):
-                prod = jnp.where(
-                    sx[j + 1 : j + 1 + F, :] == own, fx[j + 1 : j + 1 + F, cols] * mg, 0.0
-                )
-                kg[j, pl.ds(q, 1), :] = jnp.sum(prod, axis=0, keepdims=True)
-
-        krecv[0] = kg[e]
-
-        @pl.loop(1, NE)
-        def _(i):
-            to = ahead(i)
-            remote(kg.at[to], krecv.at[i], ksem.at[0], ksem.at[1], to, t).start()
+        for j in range(NE):
+            if j < KW:
+                near = sx[j + 1 : j + 1 + F, :] == sx[16 : 16 + F, :]
+                for q in range(NQ):
+                    cols = slice(q * 128, q * 128 + 128)
+                    prod = jnp.where(
+                        near, fx[j + 1 : j + 1 + F, cols] * mgx[16 : 16 + F, cols], 0.0
+                    )
+                    kg[j, q : q + 1, :] = jnp.sum(prod, axis=0, keepdims=True)
+
+            @pl.when(e == j)
+            def _():
+                krecv[j] = kg[j]
+
+            @pl.when(e != j)
+            def _():
+                remote(kg.at[j], krecv.at[e], ksem.at[0], ksem.at[1], j, t).start()
 
         wait_recv(krecv.at[1:NE], ksem.at[1])
         kred[...] = jnp.sum(krecv[...], axis=0)
-        kall[0] = kred[...]
-        korder = kall
-
-        @pl.loop(1, NE)
-        def _(i):
-            remote(kred, korder.at[i], ksem.at[2], ksem.at[3], ahead(i), t).start()
-
-        wait_recv(kall.at[1:NE], ksem.at[3])
-
-        @pl.loop(0, NE)
-        def _(i):
-            kfull[x, behind(i)] = kall[i]
-
-        @pl.loop(1, 2 * NX)
-        def _(i):
-            remote(
-                kfull.at[x], kfull.at[x], kfsem.at[0], kfsem.at[1], e, lax.rem(t + i, 2 * NX)
-            ).start()
-
-        wait_recv(kfull.at[0:3], kfsem.at[1])
-        wait_recv(fgall, fgsem.at[1])
+        kfull[x, e] = kred[...]
+        for i in range(1, NE):
+            remote(kred, kfull.at[x, e], ksem.at[2], ksem.at[3], ahead(i), t).start()
+        wait_recv(kfull.at[x, 1:NE], ksem.at[3])
+        gather_own(kfull.at[x], kfsem)
+        gather_rest(lambda xs: kfull.at[xs], kfsem)
+        wait_recv(fgall, fgsem.at[5])
         wait_send(kg.at[1:NE], ksem.at[0])
         wait_send(kg.at[1:NE], ksem.at[2])
-        wait_send(ip.at[0 : 2 * F, 0:896], kfsem.at[0])
+        wait_send(kfull.at[0:3], kfsem.at[0])
+        wait_send(kfull, kfsem.at[4])
 
     wait_recv(gg.at[1 : 2 * NX], ggsem.at[1])
     gg_out[...] = jnp.sum(gg[...], axis=0)
@@ -524,17 +570,29 @@
         for q in range(NQ):
             kg_out[:, xs * DX + q * 128 : xs * DX + q * 128 + 128] = kfull[xs, 0:KW, q, :]
 
-    store_in.wait()
-    store_out.wait()
     halo_up.wait_send()
     halo_down.wait_send()
     wait_send(sendbuf.at[CAP:SLOTS, :], asend.at[0])
-    wait_send(grecv.at[1:NE], asend.at[1])
+
+    @pl.when(c == 1)
+    def _():
+        wait_send(grecv.at[1:NE], asend.at[1])
+        share.wait_send()
+
     wait_send(rows.at[c, :, xcols], xsend.at[0])
     wait_send(rows.at[c, :, xcols], xsend.at[1])
     wait_send(rows.at[c, :, xcols], xsend.at[2])
     wait_send(rows.at[c], ssend.at[0])
-    wait_send(gpret.at[1:NE], gpsem.at[0])
+    wait_send(gpx.at[1 : 2 * NX], gpsem.at[0])
+
+    @pl.when(t == 0)
+    def _():
+        wait_send(gpret.at[1:NY], gpsem.at[2])
+
+    @pl.when(t > 0)
+    def _():
+        wait_send(gpret, gpsem.at[2])
+
     wait_send(sibrecv, sibsem.at[0])
     wait_send(r1.at[:, 0], rsem.at[0])
     wait_send(r1.at[:, 1], rsem.at[1])
@@ -553,16 +611,28 @@
     wait_send(gg.at[1 : 2 * NX], ggsem.at[0])
 
 
+def write_out(*refs):
+    copies = [pltpu.make_async_copy(refs[k], refs[5 + k], refs[10].at[k]) for k in range(5)]
+    for copy in copies:
+        copy.start()
+    for copy in copies:
+        copy.wait()
+
+
 def on_device(frames, cotangent, segment_ids, kernel, expert_ids, gates, w_in, w_out):
     vmem = pl.BlockSpec(memory_space=pltpu.VMEM)
-    anywhere = pl.BlockSpec(memory_space=pl.ANY)
+    hbm = pl.BlockSpec(memory_space=pltpu.HBM)
     dma = pltpu.SemaphoreType.DMA
     V = pltpu.VMEM
     scratch = dict(
+        frames=V((F, D), BF16),
+        cot=V((F, D), BF16),
+        seg=V((1, F), jnp.int32),
+        kern=V((KW, D), F32),
+        ids=V((2, F), jnp.int32),
+        gates=V((2, F), BF16),
         win=V((D, HS), BF16),
         wout=V((HS, D), BF16),
-        wig=V((D, HS), BF16),
-        wog=V((HS, D), BF16),
         rows=V((2, SLOTS, D), BF16),
         sendbuf=V((SLOTS, DX), BF16),
         src=V((F, DX), BF16),
@@ -578,7 +648,9 @@
         pgrad=V((SLOTS, HS), BF16),
         gacc=V((SLOTS, 128), F32),
         gpsend=V((4, 1, 128), F32),
-        gpret=V((NE, 1, 128), F32),
+        gpx=V((2 * NX, 1, 128), F32),
+        gprow=V((1, 1, 128), F32),
+        gpret=V((NY, 1, 128), F32),
         ip=V((SLOTS, D), BF16),
         sibrecv=V((2, F, D), BF16),
         cs=V((2, F, D), BF16),
@@ -594,44 +666,43 @@
         kg=V((NE, 4, 128), F32),
         krecv=V((NE, 4, 128), F32),
         kred=V((4, 128), F32),
-        kall=V((NE, 4, 128), F32),
         kfull=V((NX, NE, 4, 128), F32),
         gg=V((2 * NX, 2, 128), F32),
         posr=V((2, F, F), jnp.int32),
         posc=V((2, F, F), jnp.int32),
-        lsem=dma((4,)),
+        lsem=dma((8,)),
         hsem=dma((4,)),
         asend=dma((2,)),
         arecv=dma((4,)),
-        gsem=dma((1,)),
+        gsem=dma((3,)),
         xsend=dma((3,)),
         ssend=dma((1,)),
         fl=dma((4,)),
         fr=dma((4,)),
         fo=dma((4,)),
         fs=dma((4,)),
-        gpsem=dma((2,)),
+        gpsem=dma((4,)),
         sibsem=dma((3,)),
         rsem=dma((12,)),
         retsem=dma((3,)),
         pmsem=dma((2,)),
         mhsem=dma((4,)),
-        fgsem=dma((2,)),
+        fgsem=dma((6,)),
         ksem=dma((4,)),
-        kfsem=dma((2,)),
+        kfsem=dma((6,)),
         ggsem=dma((2,)),
     )
-    fg, kg, wig, wog, gg = pl.pallas_call(
+    made = pl.pallas_call(
         body,
         out_shape=(
-            jax.ShapeDtypeStruct((F, D), BF16),
-            jax.ShapeDtypeStruct((KW, D), F32),
-            jax.ShapeDtypeStruct((D, HS), BF16),
-            jax.ShapeDtypeStruct((HS, D), BF16),
-            jax.ShapeDtypeStruct((2, F), F32),
+            V((F, D), BF16),
+            V((KW, D), F32),
+            V((D, HS), BF16),
+            V((HS, D), BF16),
+            V((2, F), F32),
         ),
-        in_specs=[vmem] * 6 + [anywhere] * 2,
-        out_specs=(vmem, vmem, anywhere, anywhere, vmem),
+        in_specs=[hbm] * 8,
+        out_specs=(vmem,) * 5,
         scratch_shapes=list(scratch.values()),
         compiler_params=pltpu.CompilerParams(
             collective_id=0, has_side_effects=True, vmem_limit_bytes=56 * 1024 * 1024
@@ -646,6 +717,14 @@
         w_in[0],
         w_out[0],
     )
+    fg, kg, wig, wog, gg = pl.pallas_call(
+        write_out,
+        out_shape=tuple(pltpu.HBM(v.shape, v.dtype) for v in made),
+        in_specs=[vmem] * 5,
+        out_specs=(hbm,) * 5,
+        scratch_shapes=[dma((5,))],
+        compiler_params=pltpu.CompilerParams(vmem_limit_bytes=2 * 1024 * 1024),
+    )(*made)
     return fg, kg, wig[None], wog[None], gg.T
 
 

time: 97.2 us -> 88.3 us (0.908)
  local copies, waits for them, and re-layouts: 8.73 us -> 0 us
    unnamed x9 -> x0, local copies, waits for them, and re-layouts: 8.73 us -> none
    pallas_call x1 -> x2, Pallas kernels: 87.7 us -> 87.6 us  [the longest x1 85.2 us: on_device(): pl.pallas_call(body, out_shape=(V((F, D), BF16), V((KW, D), F32), V((D, H...]
where the time goes in v2:
time: 88.3 us; the launch traced here: 88.2 us
  Pallas kernels  87.6 us (99%)
    pallas_call x1, Pallas kernels, on_device(): pl.pallas_call(body, out_shape=(V((F, D), BF16), V((KW, D), F32), V((D, H...  85.2 us
    pallas_call x1, Pallas kernels, on_device(): pl.pallas_call(write_out, out_shape=tuple((pltpu.HBM(v.shape, v.dtype) fo...  2.42 us

profile of v2, /device:TPU:1, one launch (start us, length us, event | category | flops | bytes accessed | tf_op | source)
XLA Modules:
  0.0 88.2 jit_solution(4100684051334988717)
XLA Ops:
  0.6 85.2 %shard_map.119 = (bf16[128,1536]{1,0:T(8,128)(2,1)S(1)}, f32[31,1536]{1,0:T(8,128)S(1)}, bf16[1536,768]{1,0:T(8,128)(2,1)S(1)}, bf16[768,1536]{1,0:T(8,128)(2,1)S(1)}, f32[2,128]{1,0:T(2,128)S(1)}) custom-call(bf16[128,1536]{1,0:T(8,128)(2,1)} %frames_in.1, bf16[128,1536]{1,0:T(8,128)(2,1)} %cot_in.1, s32[1,128]{1,0:T(1,128)} %bitcast.11, ...), custom_call_target="tpu_custom_call" | custom-call | tf_op jit(solution)/shard_map/pallas_call | solution.py:695
  85.8 2.4 %shard_map.120 = (bf16[128,1536]{1,0:T(8,128)(2,1)}, f32[31,1536]{1,0:T(8,128)}, bf16[1536,768]{1,0:T(8,128)(2,1)}, bf16[768,1536]{1,0:T(8,128)(2,1)}, f32[2,128]{1,0:T(2,128)}) custom-call(bf16[128,1536]{1,0:T(8,128)(2,1)S(1)} %get-tuple-element.15.refs_0_, f32[31,1536]{1,0:T(8,128)S(1)} %get-tuple-element.16.refs_1_, ...), custom_call_target="tpu_custom_call" | custom-call | tf_op jit(solution)/shard_map/pallas_call | solution.py:720

commit v3 on v2

--- a/solution.py
+++ b/solution.py
@@ -29,10 +29,10 @@
     frames_in, cot_in, seg_in, kern_in, ids_in, gates_in, w_in, w_out,
     fg_out, kg_out, wig, wog, gg_out,
     frames, cot, seg, kern, ids, gates,
-    win, wout, rows, sendbuf, src, hs, hr, fx, sx, gsend, grecv, wcol,
+    win, wout, rows, sendbuf, src, hs, hr, fx, fx2, sx, gsend, grecv, wcol,
     scaled, hidden, pgrad, gacc, gpsend, gpx, gprow, gpret, ip, sibrecv, cs, r1, s2, r2, fin, ret,
-    pmg, pmr, mgx, fgall, kg, krecv, kred, kfull, gg, posr, posc,
-    lsem, hsem, asend, arecv, gsem, xsend, ssend, fl, fr, fo, fs, gpsem, sibsem, rsem,
+    pmg, pmr, mgx, fgall, kg, krecv, kz, kfull, gg, posr, posc,
+    lsem, hsem, asend, arecv, gsem, xsend, ssend, fl, fr, fs, gpsem, sibsem, rsem,
     retsem, pmsem, mhsem, fgsem, ksem, kfsem, ggsem,
 ):
     e = lax.axis_index("expert")
@@ -78,6 +78,11 @@
         pl.semaphore_signal(
             barrier, inc=1, device_id=(e, lax.rem(t + i, 2 * NX)), device_id_type=MESH
         )
+    for tt in (right, left, facing):
+        for m in range(1, NY):
+            pl.semaphore_signal(
+                barrier, inc=1, device_id=(z * NY + yt[m], tt), device_id_type=MESH
+            )
     pairs = (
         (ids_in, ids), (gates_in, gates), (seg_in, seg), (frames_in, frames), (cot_in, cot),
         (kern_in, kern), (w_in, win), (w_out, wout),
@@ -127,18 +132,19 @@
     segr = jnp.broadcast_to(seg[...], (F, F)).astype(F32)
     segc = segr.T
     sx[16 : 16 + F, :] = segc
-    hs[0, :, 0:DX] = frames[0:16, xcols]
-    hs[1, :, 0:DX] = frames[F - 16 : F, xcols]
-    hs[0, :, DX : DX + 128] = segc[0:16].astype(BF16)
-    hs[1, :, DX : DX + 128] = segc[F - 16 : F].astype(BF16)
+    ocols = full_ds(xo * DX, DX)
+    for k, rs in enumerate((slice(0, 16), slice(F - 16, F))):
+        hs[k, :, 0:DX] = frames[rs, xcols]
+        hs[k, :, DX : 2 * DX] = frames[rs, ocols]
+        hs[k, :, 2 * DX : 2 * DX + 128] = segc[rs].astype(BF16)
 
     @pl.loop(0, NQ)
     def _(q):
-        fx[16 : 16 + F, full_ds(q * 128, 128)] = frames[:, full_ds(x * DX + q * 128, 128)].astype(
-            F32
-        )
-
-    pl.semaphore_wait(barrier, NE - 1 + 2 * NX - 1)
+        tile = full_ds(q * 128, 128)
+        fx[16 : 16 + F, tile] = frames[:, full_ds(x * DX + q * 128, 128)].astype(F32)
+        fx2[16 : 16 + F, tile] = frames[:, full_ds(xo * DX + q * 128, 128)].astype(F32)
+
+    pl.semaphore_wait(barrier, NE - 1 + 2 * NX - 1 + 3 * (NY - 1))
 
     before, after = lax.rem(e + NE - 1, NE), lax.rem(e + 1, NE)
     halo_up = remote(hs.at[1], hr.at[0], hsem.at[0], hsem.at[1], after, t)
@@ -149,17 +155,17 @@
     def take_halo():
         halo_up.wait_recv()
         halo_down.wait_recv()
-        for q in range(NQ):
-            fx[0:16, 128 * q : 128 * q + 128] = hr[0, :, 128 * q : 128 * q + 128].astype(F32)
-            fx[16 + F : EXT, 128 * q : 128 * q + 128] = hr[1, :, 128 * q : 128 * q + 128].astype(
-                F32
-            )
-        sx[0:16, :] = jnp.where(e == 0, -1.0, hr[0, :, DX : DX + 128].astype(F32))
-        sx[16 + F : EXT, :] = jnp.where(e == NE - 1, -1.0, hr[1, :, DX : DX + 128].astype(F32))
-
-    def conv(ext, q, backwards):
+        for k, rs in enumerate((slice(0, 16), slice(16 + F, EXT))):
+            fx[rs, :] = hr[k, :, 0:DX].astype(F32)
+            fx2[rs, :] = hr[k, :, DX : 2 * DX].astype(F32)
+        sx[0:16, :] = jnp.where(e == 0, -1.0, hr[0, :, 2 * DX : 2 * DX + 128].astype(F32))
+        sx[16 + F : EXT, :] = jnp.where(
+            e == NE - 1, -1.0, hr[1, :, 2 * DX : 2 * DX + 128].astype(F32)
+        )
+
+    def conv(ext, xs, q, backwards):
         cols = full_ds(q * 128, 128)
-        kcols = full_ds(x * DX + q * 128, 128)
+        kcols = full_ds(xs * DX + q * 128, 128)
         acc = jnp.zeros((F, 128), F32)
         own = sx[16 : 16 + F, :]
         for j in range(KW):
@@ -167,33 +173,42 @@
             acc += jnp.where(sx[j + 1 : j + 1 + F, :] == own, ext[j + 1 : j + 1 + F, cols] * tap, 0.0)
         return acc + ext[16 : 16 + F, cols]
 
-    @pl.when(c == 0)
-    def _():
-        take_halo()
-
-        @pl.loop(0, NQ)
-        def _(q):
-            src[:, full_ds(q * 128, 128)] = conv(fx, q, False).astype(BF16)
-
-    @pl.when(c == 1)
-    def _():
-        src[...] = cot[:, xcols]
-
-    def issue(g):
+    def source(first, ext, xs):
+        @pl.when(c == 0)
+        def _():
+            if first:
+                take_halo()
+
+            @pl.loop(0, NQ)
+            def _(q):
+                src[:, full_ds(q * 128, 128)] = conv(ext, xs, q, False).astype(BF16)
+
+        @pl.when(c == 1)
+        def _():
+            src[...] = cot[:, full_ds(xs * DX, DX)]
+
+    def issue(part, xs, g):
+        cols = full_ds(xs * DX, DX)
         slot = sub + g * F
         onehot = jnp.where((posr[0] == slot) | (posr[1] == slot), 1.0, 0.0).astype(BF16)
-        gr = slice(g * F, g * F + F)
-        sendbuf[gr, :] = jnp.dot(onehot, src[...], preferred_element_type=F32).astype(BF16)
+        sendbuf[part, g * F : g * F + F, :] = jnp.dot(
+            onehot, src[...], preferred_element_type=F32
+        ).astype(BF16)
         for i in range(max(8 * g, 1), 8 * g + 8):
             blk = slice(i * CAP, i * CAP + CAP)
             remote(
-                sendbuf.at[blk, :], rows.at[c, blk, xcols], asend.at[0], arecv.at[g], ahead(i), t
+                sendbuf.at[part, blk, :], rows.at[c, blk, cols], asend.at[2 * part],
+                arecv.at[4 * part + g], ahead(i), t,
             ).start()
         if g == 0:
-            rows[c, 0:CAP, xcols] = sendbuf[0:CAP, :]
-
-    issue(0)
-    issue(1)
+            rows[c, 0:CAP, cols] = sendbuf[part, 0:CAP, :]
+
+    source(True, fx, x)
+    for g in range(4):
+        issue(0, x, g)
+    source(False, fx2, xo)
+    for g in range(4):
+        issue(1, xo, g)
 
     @pl.when(c == 1)
     def _():
@@ -213,30 +228,27 @@
         r = region(g, xs)
         remote(r, r, ssend.at[0], fs.at[g], e, sib).start()
 
+    def arrive(part, xs, g):
+        if g == 0:
+            wait_recv(rows.at[c, CAP:F, full_ds(xs * DX, DX)], arecv.at[4 * part])
+        else:
+            wait_recv(region(g, xs), arecv.at[4 * part + g])
+
     def spread(g):
-        if g == 0:
-            wait_recv(rows.at[c, CAP:F, xcols], arecv.at[0])
-        else:
-            wait_recv(region(g, x), arecv.at[g])
+        arrive(0, x, g)
         r = region(g, x)
         remote(r, r, xsend.at[0], fl.at[g], e, right).start()
         remote(r, r, xsend.at[1], fr.at[g], e, left).start()
         to_sibling(g, x)
 
     def relay(g):
-        r = region(g, xl)
-        wait_recv(r, fl.at[g])
-        lo = rows.at[c, g * F : g * F + F // 2, full_ds(xl * DX, DX)]
-        remote(lo, lo, xsend.at[2], fo.at[g], e, right).start()
+        wait_recv(region(g, xl), fl.at[g])
         to_sibling(g, xl)
-        r = region(g, xr)
-        wait_recv(r, fr.at[g])
-        hi = rows.at[c, g * F + F // 2 : g * F + F, full_ds(xr * DX, DX)]
-        remote(hi, hi, xsend.at[2], fo.at[g], e, left).start()
+        wait_recv(region(g, xr), fr.at[g])
         to_sibling(g, xr)
 
     def opposite(g):
-        wait_recv(region(g, xo), fo.at[g])
+        arrive(1, xo, g)
         to_sibling(g, xo)
 
     def from_sibling(g):
@@ -415,13 +427,13 @@
                 ).astype(BF16)
 
     spread(0)
-    issue(2)
     spread(1)
+    spread(2)
+    spread(3)
+    opposite(0)
     relay(0)
-    issue(3)
-    spread(2)
+    opposite(1)
     relay(1)
-    opposite(0)
 
     share = remote(grecv, grecv, gsem.at[1], gsem.at[2], e, sib)
 
@@ -430,9 +442,9 @@
         wait_recv(grecv.at[1:NE], gsem.at[0])
         share.start()
 
-    spread(3)
+    opposite(2)
     relay(2)
-    opposite(1)
+    opposite(3)
 
     @pl.when(c == 0)
     def _():
@@ -446,9 +458,7 @@
     from_sibling(1)
     work(0)
     relay(3)
-    opposite(2)
     inputs_grad(0)
-    opposite(3)
     scale(0)
     ring1(0)
     from_sibling(2)
@@ -461,12 +471,11 @@
     first_grad(0, 2)
     ring1(1)
     gates_on()
-    first_grad(2, 5)
+    first_grad(2, 4)
     ring2(1)
-    first_grad(5, 6)
-    second_grad(0, 2)
+    first_grad(4, 6)
     ring3(1)
-    second_grad(2, 3)
+    second_grad(0, 3)
 
     @pl.when(c == 0)
     def _():
@@ -519,7 +528,7 @@
 
         for q in range(NQ):
             tile = full_ds(x * DX + q * 128, 128)
-            fgall[:, tile] = conv(mgx, q, True).astype(BF16)
+            fgall[:, tile] = conv(mgx, x, q, True).astype(BF16)
             gather_own(fgall.at[:, tile], fgsem)
         gather_rest(lambda xs: fgall.at[:, full_ds(xs * DX, DX)], fgsem)
         wait_recv(kfull, kfsem.at[5])
@@ -541,27 +550,40 @@
                     )
                     kg[j, q : q + 1, :] = jnp.sum(prod, axis=0, keepdims=True)
 
-            @pl.when(e == j)
-            def _():
-                krecv[j] = kg[j]
-
-            @pl.when(e != j)
-            def _():
-                remote(kg.at[j], krecv.at[e], ksem.at[0], ksem.at[1], j, t).start()
-
-        wait_recv(krecv.at[1:NE], ksem.at[1])
-        kred[...] = jnp.sum(krecv[...], axis=0)
-        kfull[x, e] = kred[...]
-        for i in range(1, NE):
-            remote(kred, kfull.at[x, e], ksem.at[2], ksem.at[3], ahead(i), t).start()
-        wait_recv(kfull.at[x, 1:NE], ksem.at[3])
-        gather_own(kfull.at[x], kfsem)
-        gather_rest(lambda xs: kfull.at[xs], kfsem)
+            if j % 8 == 7:
+
+                @pl.when(y != j // 8)
+                def _():
+                    remote(
+                        kg.at[j - 7 : j + 1], krecv.at[y], ksem.at[0], ksem.at[1],
+                        z * NY + j // 8, t,
+                    ).start()
+
+                @pl.when(y == j // 8)
+                def _():
+                    krecv[y] = kg[j - 7 : j + 1]
+
+        wait_recv(krecv.at[1:NY], ksem.at[1])
+        kz[z] = jnp.sum(krecv[...], axis=0)
+        for k in range(1, NZ):
+            remote(kz.at[z], kz.at[z], ksem.at[2], ksem.at[3], zt[k] + y, t).start()
+        wait_recv(kz.at[1:NZ], ksem.at[3])
+        own = pl.ds(pl.multiple_of(y * 8, 8), 8)
+        kfull[x, own] = jnp.sum(kz[...], axis=0)
+        mine = kfull.at[x, own]
+        for k, tt in ((3, facing), (1, right), (2, left), (0, t)):
+            for m in range(0 if k else 1, NY):
+                remote(mine, mine, kfsem.at[4], kfsem.at[k], z * NY + yt[m], tt).start()
+        wait_recv(kfull.at[x, 0:24], kfsem.at[0])
+        remote(kfull.at[x], kfull.at[x], kfsem.at[6], kfsem.at[5], e, sib).start()
+        for k, xs in ((1, xl), (2, xr), (3, xo)):
+            wait_recv(kfull.at[xs], kfsem.at[k])
+            remote(kfull.at[xs], kfull.at[xs], kfsem.at[6], kfsem.at[5], e, sib).start()
         wait_recv(fgall, fgsem.at[5])
-        wait_send(kg.at[1:NE], ksem.at[0])
-        wait_send(kg.at[1:NE], ksem.at[2])
-        wait_send(kfull.at[0:3], kfsem.at[0])
-        wait_send(kfull, kfsem.at[4])
+        wait_send(krecv.at[1:NY], ksem.at[0])
+        wait_send(kz.at[1:NZ], ksem.at[2])
+        wait_send(ip.at[0:320, 0:DX], kfsem.at[4])
+        wait_send(kfull, kfsem.at[6])
 
     wait_recv(gg.at[1 : 2 * NX], ggsem.at[1])
     gg_out[...] = jnp.sum(gg[...], axis=0)
@@ -572,7 +594,8 @@
 
     halo_up.wait_send()
     halo_down.wait_send()
-    wait_send(sendbuf.at[CAP:SLOTS, :], asend.at[0])
+    wait_send(sendbuf.at[0, CAP:SLOTS, :], asend.at[0])
+    wait_send(sendbuf.at[1, CAP:SLOTS, :], asend.at[2])
 
     @pl.when(c == 1)
     def _():
@@ -581,7 +604,6 @@
 
     wait_send(rows.at[c, :, xcols], xsend.at[0])
     wait_send(rows.at[c, :, xcols], xsend.at[1])
-    wait_send(rows.at[c, :, xcols], xsend.at[2])
     wait_send(rows.at[c], ssend.at[0])
     wait_send(gpx.at[1 : 2 * NX], gpsem.at[0])
 
@@ -634,11 +656,12 @@
         win=V((D, HS), BF16),
         wout=V((HS, D), BF16),
         rows=V((2, SLOTS, D), BF16),
-        sendbuf=V((SLOTS, DX), BF16),
+        sendbuf=V((2, SLOTS, DX), BF16),
         src=V((F, DX), BF16),
-        hs=V((2, 16, DX + 128), BF16),
-        hr=V((2, 16, DX + 128), BF16),
+        hs=V((2, 16, 2 * DX + 128), BF16),
+        hr=V((2, 16, 2 * DX + 128), BF16),
         fx=V((EXT, DX), F32),
+        fx2=V((EXT, DX), F32),
         sx=V((EXT, 128), F32),
         gsend=V((4, 1, 128), F32),
         grecv=V((NE, 1, 128), F32),
@@ -664,22 +687,21 @@
         mgx=V((EXT, DX), F32),
         fgall=V((F, D), BF16),
         kg=V((NE, 4, 128), F32),
-        krecv=V((NE, 4, 128), F32),
-        kred=V((4, 128), F32),
+        krecv=V((NY, 8, 4, 128), F32),
+        kz=V((NZ, 8, 4, 128), F32),
         kfull=V((NX, NE, 4, 128), F32),
         gg=V((2 * NX, 2, 128), F32),
         posr=V((2, F, F), jnp.int32),
         posc=V((2, F, F), jnp.int32),
         lsem=dma((8,)),
         hsem=dma((4,)),
-        asend=dma((2,)),
-        arecv=dma((4,)),
+        asend=dma((3,)),
+        arecv=dma((8,)),
         gsem=dma((3,)),
-        xsend=dma((3,)),
+        xsend=dma((2,)),
         ssend=dma((1,)),
         fl=dma((4,)),
         fr=dma((4,)),
-        fo=dma((4,)),
         fs=dma((4,)),
         gpsem=dma((4,)),
         sibsem=dma((3,)),
@@ -689,7 +711,7 @@
         mhsem=dma((4,)),
         fgsem=dma((6,)),
         ksem=dma((4,)),
-        kfsem=dma((6,)),
+        kfsem=dma((7,)),
         ggsem=dma((2,)),
     )
     made = pl.pallas_call(

time: 88.3 us -> 81.5 us (0.923)
  Pallas kernels: 87.6 us -> 80.7 us
    pallas_call x1, Pallas kernels: 85.2 us -> 78.3 us  [on_device(): pl.pallas_call(body, out_shape=(V((F, D), BF16), V((KW, D), F32), V((D, H...]
where the time goes in v3:
time: 81.5 us; the launch traced here: 81.4 us
  Pallas kernels  80.7 us (99%)
    pallas_call x1, Pallas kernels, on_device(): pl.pallas_call(body, out_shape=(V((F, D), BF16), V((KW, D), F32), V((D, H...  78.3 us
    pallas_call x1, Pallas kernels, on_device(): pl.pallas_call(write_out, out_shape=tuple((pltpu.HBM(v.shape, v.dtype) fo...  2.42 us

profile of v3, /device:TPU:1, one launch (start us, length us, event | category | flops | bytes accessed | tf_op | source)
XLA Modules:
  0.0 81.4 jit_solution(4251014389047702346)
XLA Ops:
  0.6 78.3 %shard_map.119 = (bf16[128,1536]{1,0:T(8,128)(2,1)S(1)}, f32[31,1536]{1,0:T(8,128)S(1)}, bf16[1536,768]{1,0:T(8,128)(2,1)S(1)}, bf16[768,1536]{1,0:T(8,128)(2,1)S(1)}, f32[2,128]{1,0:T(2,128)S(1)}) custom-call(bf16[128,1536]{1,0:T(8,128)(2,1)} %frames_in.1, bf16[128,1536]{1,0:T(8,128)(2,1)} %cot_in.1, s32[1,128]{1,0:T(1,128)} %bitcast.11, ...), custom_call_target="tpu_custom_call" | custom-call | tf_op jit(solution)/shard_map/pallas_call | solution.py:717
  78.9 2.4 %shard_map.120 = (bf16[128,1536]{1,0:T(8,128)(2,1)}, f32[31,1536]{1,0:T(8,128)}, bf16[1536,768]{1,0:T(8,128)(2,1)}, bf16[768,1536]{1,0:T(8,128)(2,1)}, f32[2,128]{1,0:T(2,128)}) custom-call(bf16[128,1536]{1,0:T(8,128)(2,1)S(1)} %get-tuple-element.15.refs_0_, f32[31,1536]{1,0:T(8,128)S(1)} %get-tuple-element.16.refs_1_, ...), custom_call_target="tpu_custom_call" | custom-call | tf_op jit(solution)/shard_map/pallas_call | solution.py:742

commit v4 on v3

--- a/solution.py
+++ b/solution.py
@@ -11,6 +11,7 @@
 NZ, NY, NX = 8, 4, 4
 NE = NZ * NY
 F = 128
+HF = F // 2
 D = 1536
 HS = 768
 KW = 31
@@ -31,9 +32,9 @@
     frames, cot, seg, kern, ids, gates,
     win, wout, rows, sendbuf, src, hs, hr, fx, fx2, sx, gsend, grecv, wcol,
     scaled, hidden, pgrad, gacc, gpsend, gpx, gprow, gpret, ip, sibrecv, cs, r1, s2, r2, fin, ret,
-    pmg, pmr, mgx, fgall, kg, krecv, kz, kfull, gg, posr, posc,
+    mgx, fgall, kg, krecv, kz, kfull, gg, posr, posc,
     lsem, hsem, asend, arecv, gsem, xsend, ssend, fl, fr, fs, gpsem, sibsem, rsem,
-    retsem, pmsem, mhsem, fgsem, ksem, kfsem, ggsem,
+    retsem, mhsem, fgsem, ksem, kfsem, ggsem,
 ):
     e = lax.axis_index("expert")
     t = lax.axis_index("tensor")
@@ -73,12 +74,13 @@
     barrier = pltpu.get_barrier_semaphore()
 
     for i in range(1, NE):
-        pl.semaphore_signal(barrier, inc=1, device_id=(ahead(i), t), device_id_type=MESH)
+        for tt in (t, sib):
+            pl.semaphore_signal(barrier, inc=1, device_id=(ahead(i), tt), device_id_type=MESH)
     for i in range(1, 2 * NX):
         pl.semaphore_signal(
             barrier, inc=1, device_id=(e, lax.rem(t + i, 2 * NX)), device_id_type=MESH
         )
-    for tt in (right, left, facing):
+    for tt in (right, left, facing, right + sib - t, left + sib - t, facing + sib - t):
         for m in range(1, NY):
             pl.semaphore_signal(
                 barrier, inc=1, device_id=(z * NY + yt[m], tt), device_id_type=MESH
@@ -144,7 +146,7 @@
         fx[16 : 16 + F, tile] = frames[:, full_ds(x * DX + q * 128, 128)].astype(F32)
         fx2[16 : 16 + F, tile] = frames[:, full_ds(xo * DX + q * 128, 128)].astype(F32)
 
-    pl.semaphore_wait(barrier, NE - 1 + 2 * NX - 1 + 3 * (NY - 1))
+    pl.semaphore_wait(barrier, 2 * (NE - 1) + 2 * NX - 1 + 6 * (NY - 1))
 
     before, after = lax.rem(e + NE - 1, NE), lax.rem(e + 1, NE)
     halo_up = remote(hs.at[1], hr.at[0], hsem.at[0], hsem.at[1], after, t)
@@ -280,10 +282,9 @@
 
         for g in (2 * h, 2 * h + 1):
             part = jnp.sum(gacc[g * F : g * F + F, :], axis=1, keepdims=True)
-            row = jnp.sum(
+            gpsend[g] = jnp.sum(
                 jnp.where(eye, jnp.broadcast_to(part, (F, F)), 0.0), axis=0, keepdims=True
             )
-            gpsend[g] = row
 
         for tt in range(4 * h, 4 * h + 4):
 
@@ -340,68 +341,83 @@
                 gg.at[t], gg.at[t], ggsem.at[0], ggsem.at[1], e, lax.rem(t + i, 2 * NX)
             ).start()
 
-    def scale(h):
+    def scale():
         @pl.loop(0, D // 256)
         def _(n):
             cols = full_ds(n * 256, 256)
-            rh = slice(256 * h, 256 * h + 256)
-            scaled[rh, cols] = (wcol[rh, 0:1] * rows[1, rh, cols].astype(F32)).astype(BF16)
+            for h in range(4):
+                rh = slice(F * h, F * h + F)
+                scaled[rh, cols] = (wcol[rh, 0:1] * rows[1, rh, cols].astype(F32)).astype(BF16)
 
     def inputs_grad(h):
         rh = slice(256 * h, 256 * h + 256)
 
-        @pl.loop(0, 3)
-        def _(n):
-            cols = full_ds(n * 512, 512)
+        for k, xs in enumerate((xo, xr, xl, x)):
+            cols = full_ds(xs * DX, DX)
             ip[rh, cols] = lax.dot_general(
                 pgrad[rh, :], win[cols, :], (((1,), (1,)), ((), ())), preferred_element_type=F32
             ).astype(BF16)
-
-        other = full_ds((2 * h + 1 - c) * F, F)
-        remote(ip.at[other, :], sibrecv.at[h], sibsem.at[0], sibsem.at[1 + h], e, sib).start()
+            for g in (2 * h, 2 * h + 1):
+                other = pl.ds(pl.multiple_of(F * g + (1 - c) * HF, HF), HF)
+                arrived = sibsem.at[(1 if k == 0 else 5) + g]
+                remote(
+                    ip.at[other, cols], sibrecv.at[g, :, cols], sibsem.at[0], arrived, e, sib
+                ).start()
 
     def ring1(h):
-        wait_recv(sibrecv.at[h], sibsem.at[1 + h])
-        own = full_ds((2 * h + c) * F, F)
-        cs[h] = (ip[own, :].astype(F32) + sibrecv[h].astype(F32)).astype(BF16)
         oc = full_ds(xo * DX, DX)
-        remote(cs.at[h, 0:64, oc], r1.at[h, 0], rsem.at[0], rsem.at[2 + h], e, right).start()
-        remote(cs.at[h, 64:128, oc], r1.at[h, 1], rsem.at[1], rsem.at[4 + h], e, left).start()
+        wait_recv(sibrecv.at[h, :, oc], sibsem.at[1 + h])
+        own = pl.ds(pl.multiple_of(F * h + c * HF, HF), HF)
+        cs[h, :, oc] = (ip[own, oc].astype(F32) + sibrecv[h, :, oc].astype(F32)).astype(BF16)
+        remote(cs.at[h, 0:32, oc], r1.at[h, 0], rsem.at[0], rsem.at[4 + h], e, right).start()
+        remote(cs.at[h, 32:64, oc], r1.at[h, 1], rsem.at[1], rsem.at[8 + h], e, left).start()
+
+        wait_recv(sibrecv.at[h, :, 0 : 3 * DX], sibsem.at[5 + h])
+        for xs in (xr, xl, x):
+            cols = full_ds(xs * DX, DX)
+            cs[h, :, cols] = (
+                ip[own, cols].astype(F32) + sibrecv[h, :, cols].astype(F32)
+            ).astype(BF16)
 
     def ring2(h):
-        wait_recv(r1.at[h, 0], rsem.at[2 + h])
+        wait_recv(r1.at[h, 0], rsem.at[4 + h])
         rc = full_ds(xr * DX, DX)
-        s2[h, 0, 0:64, :] = (cs[h, 0:64, rc].astype(F32) + r1[h, 0].astype(F32)).astype(BF16)
-        s2[h, 0, 64:128, :] = cs[h, 64:128, rc]
-        remote(s2.at[h, 0], r2.at[h, 0], rsem.at[6], rsem.at[8 + h], e, right).start()
-        wait_recv(r1.at[h, 1], rsem.at[4 + h])
+        s2[h, 0, 0:32, :] = (cs[h, 0:32, rc].astype(F32) + r1[h, 0].astype(F32)).astype(BF16)
+        s2[h, 0, 32:64, :] = cs[h, 32:64, rc]
+        remote(s2.at[h, 0], r2.at[h, 0], rsem.at[2], rsem.at[12 + h], e, right).start()
+        wait_recv(r1.at[h, 1], rsem.at[8 + h])
         lc = full_ds(xl * DX, DX)
-        s2[h, 1, 64:128, :] = (cs[h, 64:128, lc].astype(F32) + r1[h, 1].astype(F32)).astype(BF16)
-        s2[h, 1, 0:64, :] = cs[h, 0:64, lc]
-        remote(s2.at[h, 1], r2.at[h, 1], rsem.at[7], rsem.at[10 + h], e, left).start()
+        s2[h, 1, 32:64, :] = (cs[h, 32:64, lc].astype(F32) + r1[h, 1].astype(F32)).astype(BF16)
+        s2[h, 1, 0:32, :] = cs[h, 0:32, lc]
+        remote(s2.at[h, 1], r2.at[h, 1], rsem.at[3], rsem.at[16 + h], e, left).start()
 
     def ring3(h):
-        wait_recv(r2.at[h, 0], rsem.at[8 + h])
-        wait_recv(r2.at[h, 1], rsem.at[10 + h])
+        wait_recv(r2.at[h, 0], rsem.at[12 + h])
+        wait_recv(r2.at[h, 1], rsem.at[16 + h])
         fin[h] = (
             cs[h, :, xcols].astype(F32) + r2[h, 0].astype(F32) + r2[h, 1].astype(F32)
         ).astype(BF16)
 
-        for q in range(8):
+        for q in range(4):
             blk = slice(q * CAP, q * CAP + CAP)
-            i = 16 * h + q
+            i = 8 * h + q
 
             def send():
-                to = jnp.where(c == 0, behind(i), behind(i + 8))
-                remote(
-                    fin.at[h, blk, :], ret.at[h, blk, :], retsem.at[0], retsem.at[1 + h], to, t
-                ).start()
+                to = jnp.where(c == 0, behind(i), behind(i + 4))
+                place = pl.ds(pl.multiple_of(i * CAP + c * HF, CAP), CAP)
+                for tt in (t, sib):
+                    remote(
+                        fin.at[h, blk, :], ret.at[place, :], retsem.at[0], retsem.at[1], to, tt
+                    ).start()
 
             if i == 0:
 
                 @pl.when(c == 0)
                 def _():
-                    ret[0, 0:CAP, :] = fin[0, 0:CAP, :]
+                    ret[0:CAP, :] = fin[0, 0:CAP, :]
+                    remote(
+                        fin.at[h, blk, :], ret.at[0:CAP, :], retsem.at[0], retsem.at[1], e, sib
+                    ).start()
 
                 pl.when(c == 1)(send)
             else:
@@ -433,7 +449,6 @@
     opposite(0)
     relay(0)
     opposite(1)
-    relay(1)
 
     share = remote(grecv, grecv, gsem.at[1], gsem.at[2], e, sib)
 
@@ -442,9 +457,7 @@
         wait_recv(grecv.at[1:NE], gsem.at[0])
         share.start()
 
-    opposite(2)
-    relay(2)
-    opposite(3)
+    relay(1)
 
     @pl.when(c == 0)
     def _():
@@ -457,49 +470,47 @@
     from_sibling(0)
     from_sibling(1)
     work(0)
+    opposite(2)
+    relay(2)
+    opposite(3)
     relay(3)
     inputs_grad(0)
-    scale(0)
-    ring1(0)
     from_sibling(2)
     from_sibling(3)
+    ring1(0)
+    ring1(1)
     work(1)
     ring2(0)
+    ring2(1)
     inputs_grad(1)
+    ring1(2)
+    ring1(3)
     ring3(0)
-    scale(1)
+    ring3(1)
+    ring2(2)
+    ring2(3)
+    gates_on()
     first_grad(0, 2)
-    ring1(1)
-    gates_on()
-    first_grad(2, 4)
-    ring2(1)
-    first_grad(4, 6)
-    ring3(1)
+    ring3(2)
+    ring3(3)
+    first_grad(2, 6)
+    scale()
     second_grad(0, 3)
 
     @pl.when(c == 0)
     def _():
-        wait_recv(ret.at[0, CAP:F, :], retsem.at[1])
+        wait_recv(ret.at[CAP:SLOTS, :], retsem.at[1])
 
     @pl.when(c == 1)
     def _():
-        wait_recv(ret.at[0], retsem.at[1])
-
-    wait_recv(ret.at[1], retsem.at[2])
-    picks = []
-    for h in range(2):
-        slot = lane + (2 * h + c) * F
-        picks.append(
-            jnp.where((posc[0] == slot) | (posc[1] == slot), 1.0, 0.0).astype(BF16)
-        )
-    pmg[...] = jnp.dot(picks[0], ret[0], preferred_element_type=F32) + jnp.dot(
-        picks[1], ret[1], preferred_element_type=F32
-    )
-    swap = remote(pmg, pmr, pmsem.at[0], pmsem.at[1], e, sib)
-    swap.start()
-    gates_home()
-    swap.wait_recv()
-    mgx[16 : 16 + F, :] = cot[:, xcols].astype(F32) + (pmg[...] + pmr[...])
+        wait_recv(ret, retsem.at[1])
+
+    mg = cot[:, xcols].astype(F32)
+    for g in range(4):
+        slot = lane + g * F
+        pick = jnp.where((posc[0] == slot) | (posc[1] == slot), 1.0, 0.0).astype(BF16)
+        mg += jnp.dot(pick, ret[g * F : g * F + F, :], preferred_element_type=F32)
+    mgx[16 : 16 + F, :] = mg
 
     def gather_own(r, sem):
         remote(r, r, sem.at[0], sem.at[3], e, facing).start()
@@ -523,6 +534,7 @@
         )
         up.start()
         down.start()
+        gates_home()
         up.wait_recv()
         down.wait_recv()
 
@@ -531,7 +543,8 @@
             fgall[:, tile] = conv(mgx, x, q, True).astype(BF16)
             gather_own(fgall.at[:, tile], fgsem)
         gather_rest(lambda xs: fgall.at[:, full_ds(xs * DX, DX)], fgsem)
-        wait_recv(kfull, kfsem.at[5])
+        for k, xs in ((0, x), (1, xl), (2, xr), (3, xo)):
+            wait_recv(kfull.at[xs], kfsem.at[k])
         wait_send(fgall.at[:, 0 : 3 * DX], fgsem.at[0])
         wait_send(fgall, fgsem.at[4])
         up.wait_send()
@@ -563,6 +576,7 @@
                 def _():
                     krecv[y] = kg[j - 7 : j + 1]
 
+        gates_home()
         wait_recv(krecv.at[1:NY], ksem.at[1])
         kz[z] = jnp.sum(krecv[...], axis=0)
         for k in range(1, NZ):
@@ -571,19 +585,21 @@
         own = pl.ds(pl.multiple_of(y * 8, 8), 8)
         kfull[x, own] = jnp.sum(kz[...], axis=0)
         mine = kfull.at[x, own]
-        for k, tt in ((3, facing), (1, right), (2, left), (0, t)):
-            for m in range(0 if k else 1, NY):
-                remote(mine, mine, kfsem.at[4], kfsem.at[k], z * NY + yt[m], tt).start()
+        for k, xs in ((3, xo), (1, xr), (2, xl), (0, x)):
+            for m in range(NY):
+                for cc in (0, 1):
+                    if k == 0 and m == 0 and cc == 1:
+                        continue
+                    remote(
+                        mine, mine, kfsem.at[4], kfsem.at[k], z * NY + yt[m], 2 * xs + cc
+                    ).start()
         wait_recv(kfull.at[x, 0:24], kfsem.at[0])
-        remote(kfull.at[x], kfull.at[x], kfsem.at[6], kfsem.at[5], e, sib).start()
         for k, xs in ((1, xl), (2, xr), (3, xo)):
             wait_recv(kfull.at[xs], kfsem.at[k])
-            remote(kfull.at[xs], kfull.at[xs], kfsem.at[6], kfsem.at[5], e, sib).start()
         wait_recv(fgall, fgsem.at[5])
         wait_send(krecv.at[1:NY], ksem.at[0])
         wait_send(kz.at[1:NZ], ksem.at[2])
-        wait_send(ip.at[0:320, 0:DX], kfsem.at[4])
-        wait_send(kfull, kfsem.at[6])
+        wait_send(ip.at[0:496, 0:512], kfsem.at[4])
 
     wait_recv(gg.at[1 : 2 * NX], ggsem.at[1])
     gg_out[...] = jnp.sum(gg[...], axis=0)
@@ -618,18 +634,17 @@
     wait_send(sibrecv, sibsem.at[0])
     wait_send(r1.at[:, 0], rsem.at[0])
     wait_send(r1.at[:, 1], rsem.at[1])
-    wait_send(s2.at[:, 0], rsem.at[6])
-    wait_send(s2.at[:, 1], rsem.at[7])
+    wait_send(s2.at[:, 0], rsem.at[2])
+    wait_send(s2.at[:, 1], rsem.at[3])
 
     @pl.when(c == 0)
     def _():
-        wait_send(ip.at[CAP : 2 * F, 0:DX], retsem.at[0])
+        wait_send(ip.at[CAP:SLOTS, 0:DX], retsem.at[0])
 
     @pl.when(c == 1)
     def _():
-        wait_send(ip.at[0 : 2 * F, 0:DX], retsem.at[0])
-
-    swap.wait_send()
+        wait_send(ip.at[:, 0:DX], retsem.at[0])
+
     wait_send(gg.at[1 : 2 * NX], ggsem.at[0])
 
 
@@ -675,15 +690,13 @@
         gprow=V((1, 1, 128), F32),
         gpret=V((NY, 1, 128), F32),
         ip=V((SLOTS, D), BF16),
-        sibrecv=V((2, F, D), BF16),
-        cs=V((2, F, D), BF16),
-        r1=V((2, 2, F // 2, DX), BF16),
-        s2=V((2, 2, F, DX), BF16),
-        r2=V((2, 2, F, DX), BF16),
-        fin=V((2, F, DX), BF16),
-        ret=V((2, F, DX), BF16),
-        pmg=V((F, DX), F32),
-        pmr=V((F, DX), F32),
+        sibrecv=V((4, HF, D), BF16),
+        cs=V((4, HF, D), BF16),
+        r1=V((4, 2, HF // 2, DX), BF16),
+        s2=V((4, 2, HF, DX), BF16),
+        r2=V((4, 2, HF, DX), BF16),
+        fin=V((4, HF, DX), BF16),
+        ret=V((SLOTS, DX), BF16),
         mgx=V((EXT, DX), F32),
         fgall=V((F, D), BF16),
         kg=V((NE, 4, 128), F32),
@@ -704,14 +717,13 @@
         fr=dma((4,)),
         fs=dma((4,)),
         gpsem=dma((4,)),
-        sibsem=dma((3,)),
-        rsem=dma((12,)),
-        retsem=dma((3,)),
-        pmsem=dma((2,)),
+        sibsem=dma((9,)),
+        rsem=dma((20,)),
+        retsem=dma((2,)),
         mhsem=dma((4,)),
         fgsem=dma((6,)),
         ksem=dma((4,)),
-        kfsem=dma((7,)),
+        kfsem=dma((5,)),
         ggsem=dma((2,)),
     )
     made = pl.pallas_call(

time: 81.5 us -> 79.3 us (0.973)
  Pallas kernels: 80.7 us -> 78.6 us
    pallas_call x1, Pallas kernels: 78.3 us -> 76.1 us  [on_device(): pl.pallas_call(body, out_shape=(V((F, D), BF16), V((KW, D), F32), V((D, H...]
where the time goes in v4:
time: 79.3 us; the launch traced here: 79.2 us
  Pallas kernels  78.6 us (99%)
    pallas_call x1, Pallas kernels, on_device(): pl.pallas_call(body, out_shape=(V((F, D), BF16), V((KW, D), F32), V((D, H...  76.1 us
    pallas_call x1, Pallas kernels, on_device(): pl.pallas_call(write_out, out_shape=tuple((pltpu.HBM(v.shape, v.dtype) fo...  2.42 us

profile of v4, /device:TPU:1, one launch (start us, length us, event | category | flops | bytes accessed | tf_op | source)
XLA Modules:
  0.0 79.2 jit_solution(13435691466221066036)
XLA Ops:
  0.6 76.1 %shard_map.119 = (bf16[128,1536]{1,0:T(8,128)(2,1)S(1)}, f32[31,1536]{1,0:T(8,128)S(1)}, bf16[1536,768]{1,0:T(8,128)(2,1)S(1)}, bf16[768,1536]{1,0:T(8,128)(2,1)S(1)}, f32[2,128]{1,0:T(2,128)S(1)}) custom-call(bf16[128,1536]{1,0:T(8,128)(2,1)} %frames_in.1, bf16[128,1536]{1,0:T(8,128)(2,1)} %cot_in.1, s32[1,128]{1,0:T(1,128)} %bitcast.11, ...), custom_call_target="tpu_custom_call" | custom-call | tf_op jit(solution)/shard_map/pallas_call | solution.py:729
  76.8 2.4 %shard_map.120 = (bf16[128,1536]{1,0:T(8,128)(2,1)}, f32[31,1536]{1,0:T(8,128)}, bf16[1536,768]{1,0:T(8,128)(2,1)}, bf16[768,1536]{1,0:T(8,128)(2,1)}, f32[2,128]{1,0:T(2,128)}) custom-call(bf16[128,1536]{1,0:T(8,128)(2,1)S(1)} %get-tuple-element.15.refs_0_, f32[31,1536]{1,0:T(8,128)S(1)} %get-tuple-element.16.refs_1_, ...), custom_call_target="tpu_custom_call" | custom-call | tf_op jit(solution)/shard_map/pallas_call | solution.py:754

commit v5 on v4

--- a/solution.py
+++ b/solution.py
@@ -146,6 +146,32 @@
         fx[16 : 16 + F, tile] = frames[:, full_ds(x * DX + q * 128, 128)].astype(F32)
         fx2[16 : 16 + F, tile] = frames[:, full_ds(xo * DX + q * 128, 128)].astype(F32)
 
+    def conv(ext, xs, q, backwards, lo, n):
+        cols = full_ds(q * 128, 128)
+        kcols = full_ds(xs * DX + q * 128, 128)
+        acc = ext[16 + lo : 16 + lo + n, cols]
+        own = sx[16 + lo : 16 + lo + n, :]
+        for j in range(KW):
+            tap = kern[KW - 1 - j if backwards else j, kcols].reshape(1, 128)
+            near = slice(j + 1 + lo, j + 1 + lo + n)
+            acc += jnp.where(sx[near, :] == own, ext[near, cols] * tap, 0.0)
+        return acc
+
+    @pl.when(c == 0)
+    def _():
+        for part, (ext, xs) in enumerate(((fx, x), (fx2, xo))):
+
+            @pl.loop(0, NQ)
+            def _(q):
+                src[part, 16 : F - 16, full_ds(q * 128, 128)] = conv(
+                    ext, xs, q, False, 16, F - 32
+                ).astype(BF16)
+
+    @pl.when(c == 1)
+    def _():
+        src[0] = cot[:, xcols]
+        src[1] = cot[:, ocols]
+
     pl.semaphore_wait(barrier, 2 * (NE - 1) + 2 * NX - 1 + 6 * (NY - 1))
 
     before, after = lax.rem(e + NE - 1, NE), lax.rem(e + 1, NE)
@@ -165,36 +191,24 @@
             e == NE - 1, -1.0, hr[1, :, 2 * DX : 2 * DX + 128].astype(F32)
         )
 
-    def conv(ext, xs, q, backwards):
-        cols = full_ds(q * 128, 128)
-        kcols = full_ds(xs * DX + q * 128, 128)
-        acc = jnp.zeros((F, 128), F32)
-        own = sx[16 : 16 + F, :]
-        for j in range(KW):
-            tap = kern[KW - 1 - j if backwards else j, kcols].reshape(1, 128)
-            acc += jnp.where(sx[j + 1 : j + 1 + F, :] == own, ext[j + 1 : j + 1 + F, cols] * tap, 0.0)
-        return acc + ext[16 : 16 + F, cols]
-
-    def source(first, ext, xs):
+    def source(part, ext, xs):
         @pl.when(c == 0)
         def _():
-            if first:
+            if part == 0:
                 take_halo()
 
             @pl.loop(0, NQ)
             def _(q):
-                src[:, full_ds(q * 128, 128)] = conv(ext, xs, q, False).astype(BF16)
-
-        @pl.when(c == 1)
-        def _():
-            src[...] = cot[:, full_ds(xs * DX, DX)]
+                cols = full_ds(q * 128, 128)
+                for lo in (0, F - 16):
+                    src[part, lo : lo + 16, cols] = conv(ext, xs, q, False, lo, 16).astype(BF16)
 
     def issue(part, xs, g):
         cols = full_ds(xs * DX, DX)
         slot = sub + g * F
         onehot = jnp.where((posr[0] == slot) | (posr[1] == slot), 1.0, 0.0).astype(BF16)
         sendbuf[part, g * F : g * F + F, :] = jnp.dot(
-            onehot, src[...], preferred_element_type=F32
+            onehot, src[part], preferred_element_type=F32
         ).astype(BF16)
         for i in range(max(8 * g, 1), 8 * g + 8):
             blk = slice(i * CAP, i * CAP + CAP)
@@ -205,20 +219,9 @@
         if g == 0:
             rows[c, 0:CAP, cols] = sendbuf[part, 0:CAP, :]
 
-    source(True, fx, x)
+    source(0, fx, x)
     for g in range(4):
         issue(0, x, g)
-    source(False, fx2, xo)
-    for g in range(4):
-        issue(1, xo, g)
-
-    @pl.when(c == 1)
-    def _():
-        for i in range(1, NE):
-            remote(
-                gsend.at[i // 8], grecv.at[i], asend.at[1], gsem.at[0], ahead(i), t
-            ).start()
-
     @pl.when(c == 1)
     def _():
         take_halo()
@@ -442,8 +445,21 @@
                     preferred_element_type=F32,
                 ).astype(BF16)
 
+    source(1, fx2, xo)
+    issue(1, xo, 0)
+    issue(1, xo, 1)
     spread(0)
+    issue(1, xo, 2)
+    issue(1, xo, 3)
     spread(1)
+
+    @pl.when(c == 1)
+    def _():
+        for i in range(1, NE):
+            remote(
+                gsend.at[i // 8], grecv.at[i], asend.at[1], gsem.at[0], ahead(i), t
+            ).start()
+
     spread(2)
     spread(3)
     opposite(0)
@@ -535,12 +551,19 @@
         up.start()
         down.start()
         gates_home()
+
+        @pl.loop(0, NQ)
+        def _(q):
+            fgall[16 : F - 16, full_ds(x * DX + q * 128, 128)] = conv(
+                mgx, x, q, True, 16, F - 32
+            ).astype(BF16)
+
         up.wait_recv()
         down.wait_recv()
-
         for q in range(NQ):
             tile = full_ds(x * DX + q * 128, 128)
-            fgall[:, tile] = conv(mgx, x, q, True).astype(BF16)
+            for lo in (0, F - 16):
+                fgall[lo : lo + 16, tile] = conv(mgx, x, q, True, lo, 16).astype(BF16)
             gather_own(fgall.at[:, tile], fgsem)
         gather_rest(lambda xs: fgall.at[:, full_ds(xs * DX, DX)], fgsem)
         for k, xs in ((0, x), (1, xl), (2, xr), (3, xo)):
@@ -579,14 +602,14 @@
         gates_home()
         wait_recv(krecv.at[1:NY], ksem.at[1])
         kz[z] = jnp.sum(krecv[...], axis=0)
-        for k in range(1, NZ):
+        for k in (4, 3, 5, 2, 6, 1, 7):
             remote(kz.at[z], kz.at[z], ksem.at[2], ksem.at[3], zt[k] + y, t).start()
         wait_recv(kz.at[1:NZ], ksem.at[3])
         own = pl.ds(pl.multiple_of(y * 8, 8), 8)
         kfull[x, own] = jnp.sum(kz[...], axis=0)
         mine = kfull.at[x, own]
         for k, xs in ((3, xo), (1, xr), (2, xl), (0, x)):
-            for m in range(NY):
+            for m in (2, 1, 3, 0):
                 for cc in (0, 1):
                     if k == 0 and m == 0 and cc == 1:
                         continue
@@ -672,7 +695,7 @@
         wout=V((HS, D), BF16),
         rows=V((2, SLOTS, D), BF16),
         sendbuf=V((2, SLOTS, DX), BF16),
-        src=V((F, DX), BF16),
+        src=V((2, F, DX), BF16),
         hs=V((2, 16, 2 * DX + 128), BF16),
         hr=V((2, 16, 2 * DX + 128), BF16),
         fx=V((EXT, DX), F32),

time: 79.3 us -> 78.7 us (level)
  no operation moved by 1% of the time
where the time goes in v5:
time: 78.7 us; the launch traced here: 78.6 us
  Pallas kernels  78 us (99%)
    pallas_call x1, Pallas kernels, on_device(): pl.pallas_call(body, out_shape=(V((F, D), BF16), V((KW, D), F32), V((D, H...  75.6 us
    pallas_call x1, Pallas kernels, on_device(): pl.pallas_call(write_out, out_shape=tuple((pltpu.HBM(v.shape, v.dtype) fo...  2.42 us

profile of v5, /device:TPU:1, one launch (start us, length us, event | category | flops | bytes accessed | tf_op | source)
XLA Modules:
  0.0 78.6 jit_solution(5913660733859239763)
XLA Ops:
  0.6 75.6 %shard_map.119 = (bf16[128,1536]{1,0:T(8,128)(2,1)S(1)}, f32[31,1536]{1,0:T(8,128)S(1)}, bf16[1536,768]{1,0:T(8,128)(2,1)S(1)}, bf16[768,1536]{1,0:T(8,128)(2,1)S(1)}, f32[2,128]{1,0:T(2,128)S(1)}) custom-call(bf16[128,1536]{1,0:T(8,128)(2,1)} %frames_in.1, bf16[128,1536]{1,0:T(8,128)(2,1)} %cot_in.1, s32[1,128]{1,0:T(1,128)} %bitcast.11, ...), custom_call_target="tpu_custom_call" | custom-call | tf_op jit(solution)/shard_map/pallas_call | solution.py:752
  76.2 2.4 %shard_map.120 = (bf16[128,1536]{1,0:T(8,128)(2,1)}, f32[31,1536]{1,0:T(8,128)}, bf16[1536,768]{1,0:T(8,128)(2,1)}, bf16[768,1536]{1,0:T(8,128)(2,1)}, f32[2,128]{1,0:T(2,128)}) custom-call(bf16[128,1536]{1,0:T(8,128)(2,1)S(1)} %get-tuple-element.15.refs_0_, f32[31,1536]{1,0:T(8,128)S(1)} %get-tuple-element.16.refs_1_, ...), custom_call_target="tpu_custom_call" | custom-call | tf_op jit(solution)/shard_map/pallas_call | solution.py:777

commit v6 on v5

--- a/solution.py
+++ b/solution.py
@@ -268,9 +268,9 @@
         hr_ = slice(256 * h, 256 * h + 256)
         gacc[hr_, :] = jnp.zeros((256, 128), F32)
 
-        @pl.loop(0, HS // 256)
+        @pl.loop(0, HS // 768)
         def _(n):
-            cols = full_ds(n * 256, 256)
+            cols = full_ds(n * 768, 768)
             pre = jnp.dot(rows[0, hr_, :], win[:, cols], preferred_element_type=F32)
             back = lax.dot_general(
                 rows[1, hr_, :], wout[cols, :], (((1,), (1,)), ((), ())), preferred_element_type=F32
@@ -279,7 +279,8 @@
             hid = (pre * sig).astype(BF16)
             hidden[hr_, cols] = hid
             prod = hid.astype(F32) * back
-            gacc[hr_, :] += prod[:, 0:128] + prod[:, 128:256]
+            for m in range(0, 768, 128):
+                gacc[hr_, :] += prod[:, m : m + 128]
             w = wcol[hr_, 0:1]
             pgrad[hr_, cols] = (back * w * (sig * (1.0 + pre * (1.0 - sig)))).astype(BF16)
 

time: 78.7 us -> 78.5 us (level)
  no operation moved by 1% of the time
where the time goes in v6:
time: 78.5 us; the launch traced here: 78.4 us
  Pallas kernels  77.8 us (99%)
    pallas_call x1, Pallas kernels, on_device(): pl.pallas_call(body, out_shape=(V((F, D), BF16), V((KW, D), F32), V((D, H...  75.4 us
    pallas_call x1, Pallas kernels, on_device(): pl.pallas_call(write_out, out_shape=tuple((pltpu.HBM(v.shape, v.dtype) fo...  2.42 us

profile of v6, /device:TPU:1, one launch (start us, length us, event | category | flops | bytes accessed | tf_op | source)
XLA Modules:
  0.0 78.4 jit_solution(7049153217421613983)
XLA Ops:
  0.6 75.4 %shard_map.119 = (bf16[128,1536]{1,0:T(8,128)(2,1)S(1)}, f32[31,1536]{1,0:T(8,128)S(1)}, bf16[1536,768]{1,0:T(8,128)(2,1)S(1)}, bf16[768,1536]{1,0:T(8,128)(2,1)S(1)}, f32[2,128]{1,0:T(2,128)S(1)}) custom-call(bf16[128,1536]{1,0:T(8,128)(2,1)} %frames_in.1, bf16[128,1536]{1,0:T(8,128)(2,1)} %cot_in.1, s32[1,128]{1,0:T(1,128)} %bitcast.11, ...), custom_call_target="tpu_custom_call" | custom-call | tf_op jit(solution)/shard_map/pallas_call | solution.py:753
  76.0 2.4 %shard_map.120 = (bf16[128,1536]{1,0:T(8,128)(2,1)}, f32[31,1536]{1,0:T(8,128)}, bf16[1536,768]{1,0:T(8,128)(2,1)}, bf16[768,1536]{1,0:T(8,128)(2,1)}, f32[2,128]{1,0:T(2,128)}) custom-call(bf16[128,1536]{1,0:T(8,128)(2,1)S(1)} %get-tuple-element.15.refs_0_, f32[31,1536]{1,0:T(8,128)S(1)} %get-tuple-element.16.refs_1_, ...), custom_call_target="tpu_custom_call" | custom-call | tf_op jit(solution)/shard_map/pallas_call | solution.py:778
